TPU v7x, 256 devices: a whole 4x4x8 slice. The times are simulated.
256 devices in a mesh: sta: 4 (over x), ev: 64 (over z, y, core).
Axes of the slice: x: 4, y: 4, z: 8, core: 2. Of those that a mesh axis runs over, the one named last changes fastest.
Arguments:
- traces: bfloat16 [192, 524288], P('sta', 'ev'), parts along dimension 0, may hold values from -55 to 55
- held_count: int32 [256], P('sta'), parts along dimension 0, may hold values from 2 to 62, as said below
- window_owner_table: int32 [256, 62], P('sta'), parts along dimension 0, may hold values from 0 to 2047, as said below
- pick_offset: int32 [256, 62], P(('sta', 'ev')), parts along dimension 0, may hold values from 0 to 8191
- neighbours: int32 [8192, 128], P(('sta', 'ev')), parts along dimension 0, may hold values from 0 to 287, as said below
Outputs:
- correlation: float32 [8192, 61, 128], P(('sta', 'ev')), parts along dimension 0
There are 4 independent parts, one for each index of `sta`. A program takes and returns all parts, laid end to end along the dimension named above; each array names one. Nothing has to cross between parts.
Inputs may be any that keep to these rules, and one draw needn't show every extreme that they name: `held_count`: each count is even and the counts sum to 2048; some holder holds exactly 62. `window_owner_table`: the first held_count[d] entries of row d name the events of holder d's windows; over all holders they name every event slot exactly once; entries 2i and 2i+1 of a row name positions 2j and 2j+1 of one owner; no holder names more than 2 events of one owner, and some holder names exactly that many. Other entries are not read. `pick_offset`: only the first held_count[d] entries of row d are read. `neighbours`: an event of block o names blocks o - q with q <= min(o, 8); its first neighbour lies in block o - min(o, 8).
All inputs are finite; a program needn't handle non-finite values.
Results may differ from a plain program's by a relative error of at most 0.0003.
Values may be sent and summed in bfloat16 or wider, within the bound.
No kernel may reach another device: no remote copies, remote signals or barrier semaphores. Data moves between devices by JAX's collectives and lax.ppermute only.
A program may use at most 128 MiB of HBM per device.

v0:
```python
import jax
import jax.numpy as jnp
from jax import lax
from jax.sharding import PartitionSpec as P

WIN = 256
MAXLAG = 30


def from_behind(array, axis, by):
    devices = lax.axis_size(axis)
    pairs = [(i, i + by) for i in range(devices) if 0 <= i + by < devices]
    return lax.ppermute(array, axis, pairs)


def lagged(window):
    padded = jnp.pad(window, ((0, 0), (MAXLAG, MAXLAG)))
    return jnp.stack(
        [
            padded[:, 2 * MAXLAG - lag_index : 2 * MAXLAG - lag_index + WIN]
            for lag_index in range(2 * MAXLAG + 1)
        ],
        axis=1,
    )


def body(traces, held_count, window_owner_table, pick_offset, neighbours):
    components = traces.shape[0]
    devices = lax.axis_size("ev")
    own_index = lax.axis_index("ev")
    held_slots = window_owner_table.shape[1]
    per_dev = neighbours.shape[0]
    peer_cap = 2 * ((per_dev - 2 + devices) // devices)
    flat_width = components * WIN
    next_rim = from_behind(traces[:, :WIN], "ev", -1)
    extended = jnp.concatenate([traces, next_rim], axis=1)

    def cut_window(offset):
        return lax.dynamic_slice(extended, (jnp.int32(0), offset), (components, WIN))

    windows = jax.vmap(cut_window)(pick_offset[0])
    my_row = lax.dynamic_index_in_dim(window_owner_table, own_index, 0, keepdims=False)
    held_here = lax.dynamic_index_in_dim(held_count, own_index, 0, keepdims=False)
    slots = jnp.arange(held_slots, dtype=jnp.int32)
    is_live = slots < held_here
    destination = my_row // per_dev
    earlier = (
        (slots[None, :] < slots[:, None])
        & is_live[None, :]
        & (destination[None, :] == destination[:, None])
    )
    bucket_rank = jnp.sum(earlier.astype(jnp.int32), axis=1)
    target = jnp.where(is_live, destination * peer_cap + bucket_rank, -1)
    bucket_rows = jnp.arange(devices * peer_cap, dtype=jnp.int32)
    placing = (bucket_rows[:, None] == target[None, :]).astype(jnp.bfloat16)
    bucket = jnp.dot(
        placing, windows.reshape(held_slots, flat_width), preferred_element_type=jnp.float32
    ).astype(jnp.bfloat16)
    arrived = lax.all_to_all(
        bucket.reshape(devices, peer_cap, flat_width), "ev", split_axis=0, concat_axis=0, tiled=True
    )
    all_live = slots[None, :] < held_count[:, None]
    is_mine = all_live & (window_owner_table // per_dev == own_index)
    mine_count = is_mine.astype(jnp.int32)
    before = jnp.cumsum(mine_count, axis=1) - mine_count
    wanted = own_index * per_dev + jnp.arange(per_dev, dtype=jnp.int32)
    matches = is_mine[None] & (window_owner_table[None] == wanted[:, None, None])
    source_slot = jnp.arange(devices, dtype=jnp.int32)[:, None] * peer_cap + before
    bucket_index = jnp.sum(jnp.where(matches, source_slot[None], 0), axis=(1, 2))
    picking = (bucket_rows[None, :] == bucket_index[:, None]).astype(jnp.bfloat16)
    own_block = jnp.dot(
        picking, arrived.reshape(devices * peer_cap, flat_width), preferred_element_type=jnp.float32
    )
    own_block = own_block.astype(jnp.bfloat16).reshape(per_dev, components, WIN)
    band_reach = min(8, devices // 2)
    pieces = [own_block]
    for distance in range(1, band_reach + 1):
        pieces.append(from_behind(own_block, "ev", distance))
    band_windows = jnp.concatenate(pieces, axis=0)
    energy = jnp.sum(jnp.square(band_windows.astype(jnp.float32)), axis=2)
    inverse_norm = lax.rsqrt(energy + 1e-06)
    own_norm_all = inverse_norm[:per_dev]

    def correlate_event(inputs):
        window, own_norm, paired_event = inputs
        lag_shifted_traces = lagged(window)
        remaining_peers = jnp.take(band_windows, paired_event, axis=0)
        cross_products = jnp.einsum(
            "sie,jse->sij", lag_shifted_traces, remaining_peers, preferred_element_type=jnp.float32
        )
        weight = own_norm[:, None] * jnp.take(inverse_norm, paired_event, axis=0).T
        return jnp.sum(cross_products * weight[:, None, :], axis=0)

    result = lax.map(correlate_event, (own_block, own_norm_all, neighbours))
    return result


def solution(mesh):
    in_specs = (
        P("sta", "ev"),
        P("sta"),
        P("sta", None),
        P(("sta", "ev"), None),
        P(("sta", "ev"), None),
    )
    out_specs = P(("sta", "ev"), None, None)
    return jax.shard_map(body, mesh=mesh, in_specs=in_specs, out_specs=out_specs, check_vma=False)
```

profile of v0, /device:TPU:57, one launch (start us, length us, event | category | flops | bytes accessed | tf_op | source)
XLA Modules:
  0.0 1198.0 jit_solution(2340744769696385492)
XLA Ops:
  10.0 82.6 %while.14 = (s32[]{:T(128)}, bf16[48,8448]{1,0:T(8,128)(2,1)S(1)}, s32[62,2]{0,1:T(2,128)S(1)}, bf16[62,48,256]{2,1,0:T(8,128)(2,1)S(1)}, s32[]{:T(128)}) while((s32[]{:T(128)}, bf16[48,8448]{1,0:T(8,128)(2,1)S(1)}, s32[62,2]{0,1:T(2,128)S(1)}, bf16[62,48,256]{2,1,0:T(8,128)(2,1)S(1)}, s32[]{:T(128)}) %tuple.105), condition=%wide.while_cond, body=%wide.while_body.sunk | while | flops 2 | bytes 49249 | solution.py:39
  97.7 11.3 all-to-all-start
  110.2 71.5 %all-to-all-done = bf16[64,2,12288]{2,1,0:T(2,128)(2,1)S(1)} async-done(((bf16[64,2,12288]{2,1,0:T(2,128)(2,1)}), bf16[64,2,12288]{2,1,0:T(2,128)(2,1)S(1)}, u32[]{:S(2)}, u32[]{:S(2)}) %all-to-all-start) | async-done | bytes 3145760 | tf_op jit(solution)/shard_map/all_to_all | solution.py:59
  201.1 12.4 %collective-permute-done.1 = bf16[32,48,256]{2,1,0:T(8,128)(2,1)} collective-permute-done((bf16[32,48,256]{2,1,0:T(8,128)(2,1)S(1)}, bf16[32,48,256]{2,1,0:T(8,128)(2,1)}, u32[]{:S(2)}, u32[]{:S(2)}) %collective-permute-start.1) | collective-permute-done | bytes 786464 | tf_op jit(solution)/shard_map/ppermute | solution.py:13
  218.3 37.3 %collective-permute-done.2 = bf16[32,48,256]{2,1,0:T(8,128)(2,1)S(1)} collective-permute-done((bf16[32,48,256]{2,1,0:T(8,128)(2,1)S(1)}, bf16[32,48,256]{2,1,0:T(8,128)(2,1)S(1)}, u32[]{:S(2)}, u32[]{:S(2)}) %collective-permute-start.2) | collective-permute-done | bytes 786464 | tf_op jit(solution)/shard_map/ppermute | solution.py:13
  258.7 18.1 %collective-permute-done.3 = bf16[32,48,256]{2,1,0:T(8,128)(2,1)} collective-permute-done((bf16[32,48,256]{2,1,0:T(8,128)(2,1)S(1)}, bf16[32,48,256]{2,1,0:T(8,128)(2,1)}, u32[]{:S(2)}, u32[]{:S(2)}) %collective-permute-start.3) | collective-permute-done | bytes 786464 | tf_op jit(solution)/shard_map/ppermute | solution.py:13
  280.6 26.7 %collective-permute-done.4 = bf16[32,48,256]{2,1,0:T(8,128)(2,1)S(1)} collective-permute-done((bf16[32,48,256]{2,1,0:T(8,128)(2,1)S(1)}, bf16[32,48,256]{2,1,0:T(8,128)(2,1)S(1)}, u32[]{:S(2)}, u32[]{:S(2)}) %collective-permute-start.4) | collective-permute-done | bytes 786464 | tf_op jit(solution)/shard_map/ppermute | solution.py:13
  307.3 17.6 %collective-permute-done.5 = bf16[32,48,256]{2,1,0:T(8,128)(2,1)S(1)} collective-permute-done((bf16[32,48,256]{2,1,0:T(8,128)(2,1)S(1)}, bf16[32,48,256]{2,1,0:T(8,128)(2,1)S(1)}, u32[]{:S(2)}, u32[]{:S(2)}) %collective-permute-start.5) | collective-permute-done | bytes 786464 | tf_op jit(solution)/shard_map/ppermute | solution.py:13
  324.9 16.8 %collective-permute-done.6 = bf16[32,48,256]{2,1,0:T(8,128)(2,1)S(1)} collective-permute-done((bf16[32,48,256]{2,1,0:T(8,128)(2,1)S(1)}, bf16[32,48,256]{2,1,0:T(8,128)(2,1)S(1)}, u32[]{:S(2)}, u32[]{:S(2)}) %collective-permute-start.6) | collective-permute-done | bytes 786464 | tf_op jit(solution)/shard_map/ppermute | solution.py:13
  341.8 16.8 %collective-permute-done.7 = bf16[32,48,256]{2,1,0:T(8,128)(2,1)S(1)} collective-permute-done((bf16[32,48,256]{2,1,0:T(8,128)(2,1)S(1)}, bf16[32,48,256]{2,1,0:T(8,128)(2,1)S(1)}, u32[]{:S(2)}, u32[]{:S(2)}) %collective-permute-start.7) | collective-permute-done | bytes 786464 | tf_op jit(solution)/shard_map/ppermute | solution.py:13
  358.7 12.8 %collective-permute-done.8 = bf16[32,48,256]{2,1,0:T(8,128)(2,1)S(1)} collective-permute-done((bf16[32,48,256]{2,1,0:T(8,128)(2,1)S(1)}, bf16[32,48,256]{2,1,0:T(8,128)(2,1)S(1)}, u32[]{:S(2)}, u32[]{:S(2)}) %collective-permute-start.8) | collective-permute-done | bytes 786464 | tf_op jit(solution)/shard_map/ppermute | solution.py:13
  374.4 823.6 %while.13 = (s32[]{:T(128)}, f32[32,61,128]{2,0,1:T(8,128)}, bf16[32,48,256]{2,1,0:T(8,128)(2,1)S(1)}, s32[32,128]{1,0:T(8,128)}, bf16[288,48,256]{2,1,0:T(8,128...) while((s32[]{:T(128)}, f32[32,61,128]{2,0,1:T(8,128)}, ...), condition=%wide.region_6.7_spmd, body=%wide.region_4.6_spmd.sunk | while | flops 194218496 | bytes 37495428 | solution.py:94
  378.8 10.8 stack.373
  404.6 10.8 stack.373
  430.3 10.8 stack.373
  456.0 10.8 stack.373
  481.8 10.8 stack.373
  507.5 10.8 stack.373
  533.2 10.8 stack.373
  559.0 10.8 stack.373
  584.7 10.8 stack.373
  610.4 10.8 stack.373
  636.2 10.8 stack.373
  661.9 10.8 stack.373
  687.6 10.8 stack.373
  739.1 10.8 stack.373
  764.9 10.8 stack.373
  867.8 10.8 stack.373
  919.3 10.8 stack.373
  945.0 10.8 stack.373
  970.7 10.8 stack.373
  996.5 10.8 stack.373
  (2942 shorter events, 722.0 us)
Async XLA Ops:
  0.7 8.1 collective-permute-start
  97.7 11.3 copy-start.4
  97.7 11.4 copy-start.5
  97.7 84.0 %all-to-all-start = ((bf16[64,2,12288]{2,1,0:T(2,128)(2,1)}), bf16[64,2,12288]{2,1,0:T(2,128)(2,1)S(1)}, u32[]{:S(2)}, u32[]{:S(2)}) async-start(bf16[64,2,12288]{2,1,0:T(2,128)(2,1)} %reshape.141), calls=%async_computation | async-start | bytes 6291456 | tf_op jit(solution)/shard_map/all_to_all | solution.py:59
  187.1 26.4 %collective-permute-start.1 = (bf16[32,48,256]{2,1,0:T(8,128)(2,1)S(1)}, bf16[32,48,256]{2,1,0:T(8,128)(2,1)}, u32[]{:S(2)}, u32[]{:S(2)}) collective-permute-start(bf16[32,48,256]{2,1,0:T(8,128)(2,1)S(1)} %bitcast.195), channel_id=1, source_target_pairs={{0,1},{1,2},{2,3},{3,4},{4,5},{5,6},{6,7},{7,8},{8,9},{9,10},{10,1... | collective-permute-start | bytes 2359304 | tf_op jit(solution)/shard_map/ppermute | solution.py:13
  189.2 66.4 %collective-permute-start.2 = (bf16[32,48,256]{2,1,0:T(8,128)(2,1)S(1)}, bf16[32,48,256]{2,1,0:T(8,128)(2,1)S(1)}, u32[]{:S(2)}, u32[]{:S(2)}) collective-permute-start(bf16[32,48,256]{2,1,0:T(8,128)(2,1)S(1)} %bitcast.196), channel_id=1, source_target_pairs={{0,2},{1,3},{2,4},{3,5},{4,6},{5,7},{6,8},{7,9},{8,10},{9,11},{10,... | collective-permute-start | bytes 2359304 | tf_op jit(solution)/shard_map/ppermute | solution.py:13
  192.1 84.7 %collective-permute-start.3 = (bf16[32,48,256]{2,1,0:T(8,128)(2,1)S(1)}, bf16[32,48,256]{2,1,0:T(8,128)(2,1)}, u32[]{:S(2)}, u32[]{:S(2)}) collective-permute-start(bf16[32,48,256]{2,1,0:T(8,128)(2,1)S(1)} %bitcast.197), channel_id=1, source_target_pairs={{0,3},{1,4},{2,5},{3,6},{4,7},{5,8},{6,9},{7,10},{8,11},{9,12},{10... | collective-permute-start | bytes 2359304 | tf_op jit(solution)/shard_map/ppermute | solution.py:13
  195.2 112.0 %collective-permute-start.4 = (bf16[32,48,256]{2,1,0:T(8,128)(2,1)S(1)}, bf16[32,48,256]{2,1,0:T(8,128)(2,1)S(1)}, u32[]{:S(2)}, u32[]{:S(2)}) collective-permute-start(bf16[32,48,256]{2,1,0:T(8,128)(2,1)S(1)} %bitcast.198), channel_id=1, source_target_pairs={{0,4},{1,5},{2,6},{3,7},{4,8},{5,9},{6,10},{7,11},{8,12},{9,13},{1... | collective-permute-start | bytes 2359304 | tf_op jit(solution)/shard_map/ppermute | solution.py:13
  198.3 126.6 %collective-permute-start.5 = (bf16[32,48,256]{2,1,0:T(8,128)(2,1)S(1)}, bf16[32,48,256]{2,1,0:T(8,128)(2,1)S(1)}, u32[]{:S(2)}, u32[]{:S(2)}) collective-permute-start(bf16[32,48,256]{2,1,0:T(8,128)(2,1)S(1)} %bitcast.199), channel_id=1, source_target_pairs={{0,5},{1,6},{2,7},{3,8},{4,9},{5,10},{6,11},{7,12},{8,13},{9,14},{... | collective-permute-start | bytes 2359304 | tf_op jit(solution)/shard_map/ppermute | solution.py:13
  213.5 128.3 %collective-permute-start.6 = (bf16[32,48,256]{2,1,0:T(8,128)(2,1)S(1)}, bf16[32,48,256]{2,1,0:T(8,128)(2,1)S(1)}, u32[]{:S(2)}, u32[]{:S(2)}) collective-permute-start(bf16[32,48,256]{2,1,0:T(8,128)(2,1)S(1)} %bitcast.200), channel_id=1, source_target_pairs={{0,6},{1,7},{2,8},{3,9},{4,10},{5,11},{6,12},{7,13},{8,14},{9,15},... | collective-permute-start | bytes 2359304 | tf_op jit(solution)/shard_map/ppermute | solution.py:13
  255.6 103.0 %collective-permute-start.7 = (bf16[32,48,256]{2,1,0:T(8,128)(2,1)S(1)}, bf16[32,48,256]{2,1,0:T(8,128)(2,1)S(1)}, u32[]{:S(2)}, u32[]{:S(2)}) collective-permute-start(bf16[32,48,256]{2,1,0:T(8,128)(2,1)S(1)} %bitcast.202), channel_id=1, source_target_pairs={{0,7},{1,8},{2,9},{3,10},{4,11},{5,12},{6,13},{7,14},{8,15},{9,16}... | collective-permute-start | bytes 2359304 | tf_op jit(solution)/shard_map/ppermute | solution.py:13
  276.8 94.6 %collective-permute-start.8 = (bf16[32,48,256]{2,1,0:T(8,128)(2,1)S(1)}, bf16[32,48,256]{2,1,0:T(8,128)(2,1)S(1)}, u32[]{:S(2)}, u32[]{:S(2)}) collective-permute-start(bf16[32,48,256]{2,1,0:T(8,128)(2,1)S(1)} %bitcast.203), channel_id=1, source_target_pairs={{0,8},{1,9},{2,10},{3,11},{4,12},{5,13},{6,14},{7,15},{8,16},{9,17... | collective-permute-start | bytes 2359304 | tf_op jit(solution)/shard_map/ppermute | solution.py:13
  422.8 3.1 copy-start.3
  448.5 3.1 copy-start.3
  474.2 3.1 copy-start.3
  551.4 3.1 copy-start.3
  577.2 3.1 copy-start.3
  628.7 3.1 copy-start.3
  654.4 3.1 copy-start.3
  680.1 3.1 copy-start.3
  705.9 3.1 copy-start.3
  731.6 3.1 copy-start.3
  757.3 3.1 copy-start.3
  834.5 3.1 copy-start.3
  860.3 3.1 copy-start.3
  911.7 3.1 copy-start.3
  937.5 3.1 copy-start.3
  989.0 3.1 copy-start.3
  1040.4 3.1 copy-start.3
  1143.4 3.1 copy-start.3
  1169.1 3.1 copy-start.3
  1194.8 3.1 copy-start.3
  (77 other events, 117.1 us)
where the time goes:
time: 1200 us
  local copies, waits for them, and re-layouts  799 us (67%)
  waiting for transfers between devices  230 us (19%)
  other arithmetic  67.5 us (6%)
  matrix products  46.5 us (4%)
  starting transfers between devices  37 us (3%)
  loops' own time  18.1 us (2%)
    another operation x2144, local copies, waits for them, and re-layouts, lagged(): jnp.stack([padded[:, 2 * MAXLAG - lag_index:2 * MAXLAG - lag_index + WIN]...  446 us
    ppermute x9, waiting for transfers between devices, from_behind(): return lax.ppermute(array, axis, pairs)  158 us
    gather x32, local copies, waits for them, and re-layouts, correlate_event(): remaining_peers = jnp.take(band_windows, paired_event, axis=0)  121 us
    gather x186, local copies, waits for them, and re-layouts  82.5 us
    all_to_all x1, waiting for transfers between devices, body(): lax.all_to_all(bucket.reshape(devices, peer_cap, flat_width), 'ev', split...  71.5 us
    while x192, local copies, waits for them, and re-layouts  57.3 us
    dynamic_update_slice x64, local copies, waits for them, and re-layouts, body(): result = lax.map(correlate_event, (own_block, own_norm_all, neighbours))  56.8 us
    dot_general x32, matrix products, correlate_event(): jnp.einsum('sie,jse->sij', lag_shifted_traces, remaining_peers, preferred...  43 us
  transfers between devices with their start and end apart: 10, of which 9 were waited for; matrix products, arithmetic and copies ran while one was open for 1% of the time, Pallas kernels for 0%

commit v1 on v0

v1 whole, which is shorter than its diff:
```python
import functools

import jax
import jax.numpy as jnp
from jax import lax
from jax.experimental import pallas as pl
from jax.experimental.pallas import tpu as pltpu
from jax.sharding import PartitionSpec as P

WIN = 256
MAXLAG = 30
LAGS = 2 * MAXLAG + 1
SHIFTS = 16
STEPS = 4
Q_ROWS = WIN + SHIFTS * (STEPS - 1)
LANE = 128
VMEM_LIMIT = 62 * 2**20
CHUNKS = (32, 16)


ROW = 4


def from_behind(array, axis, by):
    devices = lax.axis_size(axis)
    pairs = [(i, i + by) for i in range(devices) if 0 <= i + by < devices]
    return lax.ppermute(array, axis, pairs)


def along_row(array, by):
    row = 2 * ROW
    devices = lax.axis_size("ev")
    return lax.ppermute(array, "ev", [(i, i // row * row + (i % row + 2 * by) % row) for i in range(devices)])


def between_cores(array):
    return lax.ppermute(array, "ev", [(i, i ^ 1) for i in range(lax.axis_size("ev"))])


def cut_kernel(offset_ref, owner_ref, count_ref, traces_ref, rim_ref, *refs):
    bucket_refs, ext_ref = refs[:-1], refs[-1]
    segment = traces_ref.shape[1]
    ext_ref[:, :segment] = traces_ref[...]
    ext_ref[:, segment:] = rim_ref[...]

    def cut_pair(pair, carry):
        owner = owner_ref[2 * pair]
        windows = []
        for which in range(2):
            offset = offset_ref[2 * pair + which]
            base = pl.multiple_of(offset // LANE * LANE, LANE)
            rest = offset - base
            span = ext_ref[:, pl.ds(base, WIN + LANE)].astype(jnp.float32)
            windows.append(pltpu.roll(span, WIN + LANE - rest, axis=1)[:, :WIN])
        first = 0
        for bucket_ref in bucket_refs:
            last = first + bucket_ref.shape[1] // 2
            both = jnp.concatenate([window[first:last] for window in windows], axis=0)
            bucket_ref[owner] = both.astype(jnp.bfloat16)
            first = last
        return carry

    lax.fori_loop(0, count_ref[0] // 2, cut_pair, 0)


def cut_windows(offset, owner, count, traces, rim, devices):
    components, segment = traces.shape
    return pl.pallas_call(
        cut_kernel,
        out_shape=[jax.ShapeDtypeStruct((devices, 2 * size, WIN), jnp.bfloat16) for size in CHUNKS],
        in_specs=[pl.BlockSpec(memory_space=pltpu.SMEM)] * 3 + [pl.BlockSpec(memory_space=pltpu.VMEM)] * 2,
        out_specs=[pl.BlockSpec(memory_space=pltpu.VMEM)] * len(CHUNKS),
        scratch_shapes=[pltpu.VMEM((components, segment + WIN), jnp.bfloat16)],
        compiler_params=pltpu.CompilerParams(vmem_limit_bytes=VMEM_LIMIT),
        name="cut_windows",
    )(offset, owner, count, traces, rim)


def pick_kernel(source_ref, arrived_ref, *refs):
    own_ref, rows_ref = refs[-2:]
    components, events, _ = own_ref.shape
    for event in range(events):
        source = source_ref[event]
        pair = arrived_ref[source // 2].astype(jnp.float32)
        window = jnp.where(source % 2 == 0, pair[:components], pair[components:])
        for part in range(WIN // LANE):
            rows_ref[part, pl.ds(event, components, stride=events), :] = window[:, part * LANE : (part + 1) * LANE]
    for component in range(components):
        for part in range(WIN // LANE):
            own_ref[component, :, part * LANE : (part + 1) * LANE] = rows_ref[
                part, component * events : (component + 1) * events, :
            ].astype(jnp.bfloat16)


def pick_own(source, arrived, events, after):
    components = arrived.shape[1] // 2
    return pl.pallas_call(
        pick_kernel,
        out_shape=jax.ShapeDtypeStruct((components, events, WIN), jnp.bfloat16),
        in_specs=[pl.BlockSpec(memory_space=pltpu.SMEM), pl.BlockSpec(memory_space=pltpu.VMEM)]
        + [pl.BlockSpec(memory_space=pl.ANY)] * len(after),
        out_specs=pl.BlockSpec(memory_space=pltpu.VMEM),
        scratch_shapes=[pltpu.VMEM((WIN // LANE, components * events, LANE), jnp.float32)],
        compiler_params=pltpu.CompilerParams(vmem_limit_bytes=32 * 2**20),
        name="pick_own",
    )(source, arrived, *after)


def shift_kernel(own_ref, q_ref, padded_ref, quad_ref):
    per_lane = LANE // own_ref.shape[1]
    margin = 40
    quads = quad_ref.shape[0]
    block = lax.broadcasted_iota(jnp.int32, (1, LANE), 1) // own_ref.shape[1]
    padded_ref[:margin, :] = jnp.zeros((margin, LANE), jnp.float32)
    tail = padded_ref.shape[0] - margin - WIN
    padded_ref[margin + WIN :, :] = jnp.zeros((tail, LANE), jnp.float32)
    for step in range(own_ref.shape[0]):
        window = own_ref[step].astype(jnp.float32)
        window = jnp.concatenate([window] * per_lane, axis=0)
        for part in range(WIN // LANE):
            padded_ref[margin + part * LANE : margin + (part + 1) * LANE, :] = window[
                :, part * LANE : (part + 1) * LANE
            ].T
        first = margin - 16 - 18
        quad = padded_ref[first : first + quads, :]
        for shift in range(1, per_lane):
            quad = jnp.where(block == shift, padded_ref[first - shift : first - shift + quads, :], quad)
        quad_ref[...] = quad
        for group in range(SHIFTS // per_lane):
            begin = 16 - per_lane * group
            q_ref[step, :, group * LANE : (group + 1) * LANE] = quad_ref[begin : begin + Q_ROWS, :].astype(
                jnp.bfloat16
            )


def shifted(own, batch=4):
    components, events, _ = own.shape
    width = SHIFTS * events
    return pl.pallas_call(
        shift_kernel,
        out_shape=jax.ShapeDtypeStruct((components, Q_ROWS, width), jnp.bfloat16),
        grid=(components // batch,),
        in_specs=[pl.BlockSpec((batch, events, WIN), lambda c: (c, 0, 0))],
        out_specs=pl.BlockSpec((batch, Q_ROWS, width), lambda c: (c, 0, 0)),
        scratch_shapes=[pltpu.VMEM((328, LANE), jnp.float32), pltpu.VMEM((320, LANE), jnp.float32)],
        compiler_params=pltpu.CompilerParams(vmem_limit_bytes=32 * 2**20),
        cost_estimate=pl.CostEstimate(flops=0, bytes_accessed=components * Q_ROWS * width * 4, transcendentals=0),
        name="shifted",
    )(own)


def accumulate(q_ref, pieces, band_ref, acc_ref):
    batch, events, _ = pieces[0].shape
    width = q_ref.shape[2]
    same, other = pieces[:-1], pieces[-1]
    for c in range(batch):
        for k in range(len(same)):
            band_ref[2 * k * events : (2 * k + 1) * events, :] = same[k][c]
        for k in range(other.shape[0]):
            band_ref[(2 * k + 1) * events : (2 * k + 2) * events, :] = other[k, c]
        band = band_ref[...].astype(jnp.float32)
        row_norm = lax.rsqrt(jnp.sum(band * band, axis=1, keepdims=True) + 1e-06)
        own = q_ref[c, :, :LANE].astype(jnp.float32)
        lane_norm = lax.rsqrt(jnp.sum(own * own, axis=0, keepdims=True) + 1e-06)
        weight = row_norm * lane_norm
        weight = jnp.concatenate([weight, weight], axis=1)
        for m in range(STEPS):
            begin = SHIFTS * (STEPS - 1 - m)
            for half in range(width // 256):
                products = jnp.dot(
                    band_ref[...],
                    q_ref[c, begin : begin + WIN, half * 256 : (half + 1) * 256],
                    preferred_element_type=jnp.float32,
                )
                place = m * width + half * 256
                acc_ref[:, place : place + 256] += products * weight


def partial_kernel(count, q_ref, *refs):
    pieces, (acc_ref, band_ref) = refs[:count], refs[-2:]

    @pl.when(pl.program_id(0) == 0)
    def _():
        acc_ref[...] = jnp.zeros_like(acc_ref)

    accumulate(q_ref, pieces, band_ref, acc_ref)


def final_kernel(neighbours_ref, before_ref, q_ref, *refs):
    pieces, (out_ref, band_ref, acc_ref, turned_ref) = refs[:-4], refs[-4:]
    events = pieces[0].shape[1]
    rows = band_ref.shape[0]
    step = pl.program_id(0)

    @pl.when(step == 0)
    def _():
        acc_ref[...] = before_ref[...]

    accumulate(q_ref, pieces, band_ref, acc_ref)

    @pl.when(step == pl.num_programs(0) - 1)
    def _():
        for column in range(acc_ref.shape[1] // LANE):
            for tile in range(turned_ref.shape[0]):
                first, last = tile * LANE, min((tile + 1) * LANE, rows)
                turned_ref[tile, column * LANE : (column + 1) * LANE, : last - first] = acc_ref[
                    first:last, column * LANE : (column + 1) * LANE
                ].T
        lags = STEPS * SHIFTS
        row = lax.broadcasted_iota(jnp.int32, (rows, neighbours_ref.shape[1]), 0)
        for event in range(events):
            sums = jnp.concatenate(
                [turned_ref[tile, pl.ds(event, lags, stride=events), :] for tile in range(turned_ref.shape[0])], axis=1
            )[:, :rows]
            high = sums.astype(jnp.bfloat16)
            low = (sums - high.astype(jnp.float32)).astype(jnp.bfloat16)
            chosen = (row == neighbours_ref[event : event + 1, :]).astype(jnp.bfloat16)
            both = jnp.dot(jnp.concatenate([high, low], axis=0), chosen, preferred_element_type=jnp.float32)
            total = both[:lags] + both[lags:]
            out_ref[pl.ds(event, LAGS, stride=events), :] = total[:LAGS]


def piece_specs(pieces, batch):
    same, other = pieces[:-1], pieces[-1]
    return [pl.BlockSpec((batch, *x.shape[1:]), lambda c: (c, 0, 0)) for x in same] + [
        pl.BlockSpec((other.shape[0], batch, *other.shape[2:]), lambda c: (0, c, 0, 0))
    ]


def correlate_partial(q, pieces, after, batch=4):
    components, events, _ = pieces[0].shape
    rows = (len(pieces) - 1 + pieces[-1].shape[0]) * events
    width = q.shape[2]
    return pl.pallas_call(
        functools.partial(partial_kernel, len(pieces)),
        out_shape=jax.ShapeDtypeStruct((rows, STEPS * width), jnp.float32),
        grid=(components // batch,),
        in_specs=[pl.BlockSpec((batch, Q_ROWS, width), lambda c: (c, 0, 0))]
        + piece_specs(pieces, batch)
        + [pl.BlockSpec(memory_space=pl.ANY)] * len(after),
        out_specs=pl.BlockSpec((rows, STEPS * width), lambda c: (0, 0)),
        scratch_shapes=[pltpu.VMEM((rows, WIN), jnp.bfloat16)],
        compiler_params=pltpu.CompilerParams(vmem_limit_bytes=VMEM_LIMIT),
        cost_estimate=pl.CostEstimate(
            flops=2 * components * rows * WIN * STEPS * width, bytes_accessed=12 * 2**20, transcendentals=0
        ),
        name="correlate_partial",
    )(q, *pieces, *after)


def correlate_final(neighbours, before, q, pieces, batch=4):
    components, events, _ = pieces[0].shape
    rows = (len(pieces) - 1 + pieces[-1].shape[0]) * events
    width = q.shape[2]
    k = neighbours.shape[1]
    tiles = (rows + LANE - 1) // LANE
    sums = pl.pallas_call(
        final_kernel,
        out_shape=jax.ShapeDtypeStruct((LAGS * events, k), jnp.float32),
        grid=(components // batch,),
        in_specs=[
            pl.BlockSpec((events, k), lambda c: (0, 0)),
            pl.BlockSpec((rows, STEPS * width), lambda c: (0, 0)),
            pl.BlockSpec((batch, Q_ROWS, width), lambda c: (c, 0, 0)),
        ]
        + piece_specs(pieces, batch),
        out_specs=pl.BlockSpec((LAGS * events, k), lambda c: (0, 0)),
        scratch_shapes=[
            pltpu.VMEM((rows, WIN), jnp.bfloat16),
            pltpu.VMEM((rows, STEPS * width), jnp.float32),
            pltpu.VMEM((tiles, STEPS * width, LANE), jnp.float32),
        ],
        compiler_params=pltpu.CompilerParams(vmem_limit_bytes=VMEM_LIMIT),
        cost_estimate=pl.CostEstimate(
            flops=2 * components * rows * WIN * STEPS * width, bytes_accessed=12 * 2**20, transcendentals=0
        ),
        name="correlate_final",
    )(neighbours, before, q, *pieces)
    return jnp.transpose(sums.reshape(LAGS, events, k), (1, 0, 2))


def choose_kernel(count, core_ref, *refs):
    blocks, (sent_ref, held_ref, came, went) = refs[:count], refs[-4:]
    for core in range(2):

        @pl.when(core_ref[0] == core)
        def _(core=core):
            arriving = [
                pltpu.make_async_copy(blocks[k + core], held_ref.at[k], came.at[k]) for k in range(count - 1)
            ]
            leaving = [
                pltpu.make_async_copy(held_ref.at[k], sent_ref.at[k], went.at[k]) for k in range(count - 1)
            ]
            for copy in arriving:
                copy.start()
            for k in range(count - 1):
                arriving[k].wait()
                leaving[k].start()
            for copy in leaving:
                copy.wait()


def exchange(core, blocks, after):
    sent = pl.pallas_call(
        functools.partial(choose_kernel, len(blocks)),
        out_shape=jax.ShapeDtypeStruct((len(blocks) - 1, *blocks[0].shape), blocks[0].dtype),
        in_specs=[pl.BlockSpec(memory_space=pltpu.SMEM)]
        + [pl.BlockSpec(memory_space=pl.ANY)] * (len(blocks) + len(after)),
        out_specs=pl.BlockSpec(memory_space=pl.ANY),
        scratch_shapes=[pltpu.VMEM((len(blocks) - 1, *blocks[0].shape), blocks[0].dtype)]
        + [pltpu.SemaphoreType.DMA((len(blocks) - 1,))] * 2,
        compiler_params=pltpu.CompilerParams(vmem_limit_bytes=32 * 2**20),
        name="exchange",
    )(core, *blocks, *after)
    return between_cores(sent)


def hold(array, after):
    return pl.pallas_call(
        lambda *refs: None,
        out_shape=jax.ShapeDtypeStruct(array.shape, array.dtype),
        in_specs=[pl.BlockSpec(memory_space=pl.ANY)] * (1 + len(after)),
        out_specs=pl.BlockSpec(memory_space=pl.ANY),
        input_output_aliases={0: 0},
        name="hold",
    )(array, *after)


def along_rows(y, own, above):
    sent = [jnp.where(y + by >= ROW, above, own) for by in range(1, ROW)]
    return [along_row(x, by) for by, x in enumerate(sent, 1)], sent


def spread(array):
    return lax.all_to_all(array, "ev", split_axis=0, concat_axis=0, tiled=True)


def body(traces, held_count, window_owner_table, pick_offset, neighbours):
    devices = lax.axis_size("ev")
    own_index = lax.axis_index("ev")
    held_slots = window_owner_table.shape[1]
    per_dev = neighbours.shape[0]
    next_rim = from_behind(traces[:, :WIN], "ev", -1)

    my_row = lax.dynamic_index_in_dim(window_owner_table, own_index, 0, keepdims=False)
    held_here = lax.dynamic_index_in_dim(held_count, own_index, 0, keepdims=True)
    buckets = cut_windows(pick_offset[0], my_row // per_dev, held_here, traces, next_rim, devices)

    slots = jnp.arange(held_slots, dtype=jnp.int32)
    all_live = slots[None, :] < held_count[:, None]
    wanted = own_index * per_dev + jnp.arange(per_dev, dtype=jnp.int32)
    matches = all_live[None] & (window_owner_table[None] == wanted[:, None, None])
    place = 2 * jnp.arange(devices, dtype=jnp.int32)[:, None] + slots[None, :] % 2
    source = jnp.sum(jnp.where(matches, place[None], 0), axis=(1, 2))

    y, core = own_index // 2 % ROW, (own_index % 2)[None]

    first = pick_own(source, spread(buckets[0]), per_dev, ())
    first_above = from_behind(first, "ev", 2 * ROW)
    first_q = shifted(first)
    arrived = spread(hold(buckets[1], [first_above]))
    row, _ = along_rows(y, first, first_above)
    blocks = [first, *row, first_above]
    first_pieces = blocks + [exchange(core, blocks, [first_q])]

    second = pick_own(source, arrived, per_dev, ())
    second_above = from_behind(second, "ev", 2 * ROW)
    second_q = shifted(second)
    row, sent = along_rows(y, second, second_above)
    sums = correlate_partial(first_q, first_pieces, [*sent, second_q])
    blocks = [second, *row, second_above]
    second_pieces = blocks + [exchange(core, blocks, [sums])]
    return correlate_final(neighbours, sums, second_q, second_pieces)


def solution(mesh):
    in_specs = (
        P("sta", "ev"),
        P("sta"),
        P("sta", None),
        P(("sta", "ev"), None),
        P(("sta", "ev"), None),
    )
    out_specs = P(("sta", "ev"), None, None)
    return jax.shard_map(body, mesh=mesh, in_specs=in_specs, out_specs=out_specs, check_vma=False)
```

time: 1200 us -> 187 us (0.16)
  the two profiles are of different devices: /device:TPU:57 before, /device:TPU:35 now
where the time goes in v1:
time: 187 us; the launch traced here: 186 us
  waiting for transfers between devices  87.3 us (47%)
  starting transfers between devices  45.1 us (24%)
  Pallas kernels  42.5 us (23%)
  local copies, waits for them, and re-layouts  7.29 us (4%)
  other arithmetic  3.81 us (2%)
    all_to_all x2, waiting for transfers between devices, spread(): return lax.all_to_all(array, 'ev', split_axis=0, concat_axis=0, tiled=True)  49.4 us
    all_to_all x2, starting transfers between devices, spread(): return lax.all_to_all(array, 'ev', split_axis=0, concat_axis=0, tiled=True)  24.8 us
    ppermute x6, waiting for transfers between devices, along_row(): lax.ppermute(array, 'ev', [(i, i // row * row + (i % row + 2 * by) % row)...  18.6 us
    ppermute x3, waiting for transfers between devices, from_behind(): return lax.ppermute(array, axis, pairs)  16.9 us
    pallas_call x1, Pallas kernels, correlate_partial(): pl.pallas_call(functools.partial(partial_kernel, len(pieces)), out_shape=...  14.8 us
    pallas_call x1, Pallas kernels, correlate_final(): pl.pallas_call(final_kernel, out_shape=jax.ShapeDtypeStruct((LAGS * event...  13.4 us
    ppermute x6, starting transfers between devices, along_row(): lax.ppermute(array, 'ev', [(i, i // row * row + (i % row + 2 * by) % row)...  7.32 us
    ppermute x2, starting transfers between devices, between_cores(): lax.ppermute(array, 'ev', [(i, i ^ 1) for i in range(lax.axis_size('ev'))])  6.65 us
  transfers between devices with their start and end apart: 13, of which 7 were waited for; matrix products, arithmetic and copies ran while one was open for 2% of the time, Pallas kernels for 13%

profile of v1, /device:TPU:35, one launch (start us, length us, event | category | flops | bytes accessed | tf_op | source)
XLA Modules:
  0.0 186.3 jit_solution(1116449678141124102)
XLA Ops:
  0.7 2.6 %collective-permute-start = (bf16[48,256]{1,0:T(8,128)(2,1)S(1)}, bf16[48,256]{1,0:T(8,128)(2,1)S(1)}, u32[]{:S(2)}, u32[]{:S(2)}) collective-permute-start(bf16[48,256]{1,0:T(8,128)(2,1)S(1)} %slice.3), channel_id=1, source_target_pairs={{1,0},{2,1},{3,2},{4,3},{5,4},{6,5},{7,6},{8,7},{9,8},{10,9},{11,1... | collective-permute-start | bytes 73736 | tf_op jit(solution)/shard_map/ppermute | solution.py:27
  3.3 1.3 and_select_fusion.owner_ref
  4.6 1.2 dynamic_slice.9.count_ref
  6.6 3.7 %cut_windows.1 = (bf16[64,64,256]{2,1,0:T(8,128)(2,1)}, bf16[64,32,256]{2,1,0:T(8,128)(2,1)}) custom-call(s32[62]{0:T(128)} %bitcast.13, s32[62]{0:T(128)} %and_select_fusion.owner_ref, s32[1]{0:T(128)} %dynamic_slice.9.count_ref, bf16[48,8192]{1,0:T(8,128)(2,1)} %traces_ref.1, bf16[48,256]{1,0:T(8,128)(2,1)} %copy-done.15), custom_call_target="tpu_custom_call" | custom-call | tf_op jit(solution)/shard_map/cut_windows/pallas_call | solution.py:68
  10.3 16.4 %all-to-all-start = ((bf16[64,64,256]{2,1,0:T(8,128)(2,1)}), bf16[64,64,256]{2,1,0:T(8,128)(2,1)S(1)}, u32[]{:S(2)}, u32[]{:S(2)}) async-start(bf16[64,64,256]{2,1,0:T(8,128)(2,1)} %get-tuple-element.7), calls=%async_computation | async-start | bytes 4194304 | tf_op jit(solution)/shard_map/all_to_all | solution.py:335
  27.5 49.4 %all-to-all-done.arrived_ref = bf16[64,64,256]{2,1,0:T(8,128)(2,1)S(1)} async-done(((bf16[64,64,256]{2,1,0:T(8,128)(2,1)}), bf16[64,64,256]{2,1,0:T(8,128)(2,1)S(1)}, u32[]{:S(2)}, u32[]{:S(2)}) %all-to-all-start) | async-done | bytes 2097184 | tf_op jit(solution)/shard_map/all_to_all | solution.py:335
  76.9 1.8 pick_own.2.own_ref.refs_0_
  78.7 1.9 %collective-permute-start.1 = (bf16[32,32,256]{2,1,0:T(8,128)(2,1)S(1)}, bf16[32,32,256]{2,1,0:T(8,128)(2,1)S(1)}, u32[]{:S(2)}, u32[]{:S(2)}) collective-permute-start(bf16[32,32,256]{2,1,0:T(8,128)(2,1)S(1)} %pick_own.2.own_ref.refs_0_), channel_id=1, source_target_pairs={{0,8},{1,9},{2,10},{3,11},{4,12},{5,13},{6,14},{7,15},{8,16},{9,17... | collective-permute-start | bytes 1572872 | tf_op jit(solution)/shard_map/ppermute | solution.py:27
  80.7 12.8 %collective-permute-done.1.refs_4_.refs_1_ = bf16[32,32,256]{2,1,0:T(8,128)(2,1)S(1)} collective-permute-done((bf16[32,32,256]{2,1,0:T(8,128)(2,1)S(1)}, bf16[32,32,256]{2,1,0:T(8,128)(2,1)S(1)}, u32[]{:S(2)}, u32[]{:S(2)}) %collective-permute-start.1) | collective-permute-done | bytes 524320 | tf_op jit(solution)/shard_map/ppermute | solution.py:27
  93.5 1.1 broadcast_select_fusion
  94.6 1.0 collective-permute-start.2
  95.6 2.4 %collective-permute-start.3 = (bf16[32,32,256]{2,1,0:T(8,128)(2,1)}, bf16[32,32,256]{2,1,0:T(8,128)(2,1)}, u32[]{:S(2)}, u32[]{:S(2)}) collective-permute-start(bf16[32,32,256]{2,1,0:T(8,128)(2,1)} %get-tuple-element.10), channel_id=1, source_target_pairs={{0,4},{1,5},{2,6},{3,7},{4,0},{5,1},{6,2},{7,3},{8,12},{9,13},{10,... | collective-permute-start | bytes 1572872 | tf_op jit(solution)/shard_map/ppermute | solution.py:33
  98.0 1.2 collective-permute-start.4
  99.2 8.3 %all-to-all-start.1 = ((bf16[64,32,256]{2,1,0:T(8,128)(2,1)}), bf16[64,32,256]{2,1,0:T(8,128)(2,1)S(1)}, u32[]{:S(2)}, u32[]{:S(2)}) async-start(bf16[64,32,256]{2,1,0:T(8,128)(2,1)} %hold.1), calls=%async_computation.1 | async-start | bytes 2097152 | tf_op jit(solution)/shard_map/all_to_all | solution.py:335
  107.6 3.3 %shifted.2.refs_5_.q_ref = bf16[32,304,512]{2,1,0:T(8,128)(2,1)S(1)} custom-call(bf16[32,32,256]{2,1,0:T(8,128)(2,1)S(1)} %pick_own.2.own_ref.refs_0_), custom_call_target="tpu_custom_call" | custom-call | bytes 19922944 | tf_op jit(solution)/shard_map/shifted/pallas_call | solution.py:139
  110.9 16.7 %collective-permute-done.3.refs_2_ = bf16[32,32,256]{2,1,0:T(8,128)(2,1)} collective-permute-done((bf16[32,32,256]{2,1,0:T(8,128)(2,1)}, bf16[32,32,256]{2,1,0:T(8,128)(2,1)}, u32[]{:S(2)}, u32[]{:S(2)}) %collective-permute-start.3) | collective-permute-done | bytes 524320 | tf_op jit(solution)/shard_map/ppermute | solution.py:33
  127.6 1.9 collective-permute-done.4.refs_3_
  129.5 2.5 %exchange.2 = bf16[4,32,32,256]{3,2,1,0:T(8,128)(2,1)} custom-call(s32[1]{0:T(128)} %bitcast.2.core_ref, bf16[32,32,256]{2,1,0:T(8,128)(2,1)S(1)} %pick_own.2.own_ref.refs_0_, bf16[32,32,256]{2,1,0:T(8,128)(2,1)S(1)} %collective-permute-done.2.refs_1_, bf16[32,32,256]{2,1,0:T(8,128)(2,1)} %collective-permute-done.3.refs_2_, ...), custom_call_target="tpu_custom_call" | custom-call | tf_op jit(solution)/shard_map/exchange/pallas_call | solution.py:304
  132.0 4.1 %collective-permute-start.5 = (bf16[4,32,32,256]{3,2,1,0:T(8,128)(2,1)}, bf16[4,32,32,256]{3,2,1,0:T(8,128)(2,1)}, u32[]{:S(2)}, u32[]{:S(2)}) collective-permute-start(bf16[4,32,32,256]{3,2,1,0:T(8,128)(2,1)} %exchange.2), channel_id=1, source_target_pairs={{0,1},{1,0},{2,3},{3,2},{4,5},{5,4},{6,7},{7,6},{8,9},{9,8},{10,11... | collective-permute-start | bytes 6291464 | tf_op jit(solution)/shard_map/ppermute | solution.py:37
  136.1 1.2 pick_own.3.own_ref.refs_0_
  137.3 1.9 %collective-permute-start.6 = (bf16[16,32,256]{2,1,0:T(8,128)(2,1)S(1)}, bf16[16,32,256]{2,1,0:T(8,128)(2,1)S(1)}, u32[]{:S(2)}, u32[]{:S(2)}) collective-permute-start(bf16[16,32,256]{2,1,0:T(8,128)(2,1)S(1)} %pick_own.3.own_ref.refs_0_), channel_id=1, source_target_pairs={{0,8},{1,9},{2,10},{3,11},{4,12},{5,13},{6,14},{7,15},{8,16},{9,17... | collective-permute-start | bytes 786440 | tf_op jit(solution)/shard_map/ppermute | solution.py:27
  139.2 1.6 shifted.3.refs_9_.q_ref
  140.9 2.3 %copy-done.2 = bf16[16,304,512]{2,1,0:T(8,128)(2,1)} copy-done((bf16[16,304,512]{2,1,0:T(8,128)(2,1)}, bf16[16,304,512]{2,1,0:T(8,128)(2,1)S(1)}, u32[]{:S(2)}) %copy-start.2) | copy-done | bytes 4980760
  143.2 3.9 %collective-permute-done.6.refs_4_ = bf16[16,32,256]{2,1,0:T(8,128)(2,1)S(1)} collective-permute-done((bf16[16,32,256]{2,1,0:T(8,128)(2,1)S(1)}, bf16[16,32,256]{2,1,0:T(8,128)(2,1)S(1)}, u32[]{:S(2)}, u32[]{:S(2)}) %collective-permute-start.6) | collective-permute-done | bytes 262176 | tf_op jit(solution)/shard_map/ppermute | solution.py:27
  147.1 0.8 broadcast_select_fusion.3
  147.9 1.8 collective-permute-start.8
  149.7 0.9 collective-permute-start.9
  150.6 14.8 %correlate_partial.1.refs_5_.before_ref = f32[288,2048]{1,0:T(8,128)} custom-call(bf16[32,304,512]{2,1,0:T(8,128)(2,1)} %copy-done, bf16[32,32,256]{2,1,0:T(8,128)(2,1)} %copy-done.1, bf16[32,32,256]{2,1,0:T(8,128)(2,1)} %copy-done.8, bf16[32,32,256]{2,1,0:T(8,128)(2,1)} %collective-permute-done.3.refs_2_, ...), custom_call_target="tpu_custom_call" | custom-call | flops 9663676416 | bytes 12582912 | tf_op jit(solution)/shard_map/correlate_partial/pallas_call | solution.py:234
  165.5 1.8 copy-done.6
  168.0 2.5 %collective-permute-start.10 = (bf16[4,16,32,256]{3,2,1,0:T(8,128)(2,1)S(1)}, bf16[4,16,32,256]{3,2,1,0:T(8,128)(2,1)}, u32[]{:S(2)}, u32[]{:S(2)}) collective-permute-start(bf16[4,16,32,256]{3,2,1,0:T(8,128)(2,1)S(1)} %exchange.3), channel_id=1, source_target_pairs={{0,1},{1,0},{2,3},{3,2},{4,5},{5,4},{6,7},{7,6},{8,9},{9,8},{10,11... | collective-permute-start | bytes 3145736 | tf_op jit(solution)/shard_map/ppermute | solution.py:37
  170.5 2.4 %collective-permute-done.10.refs_5_ = bf16[4,16,32,256]{3,2,1,0:T(8,128)(2,1)} collective-permute-done((bf16[4,16,32,256]{3,2,1,0:T(8,128)(2,1)S(1)}, bf16[4,16,32,256]{3,2,1,0:T(8,128)(2,1)}, u32[]{:S(2)}, u32[]{:S(2)}) %collective-permute-start.10) | collective-permute-done | bytes 1048608 | tf_op jit(solution)/shard_map/ppermute | solution.py:37
  172.9 13.4 %correlate_final.1 = f32[1952,128]{1,0:T(8,128)} custom-call(s32[32,128]{1,0:T(8,128)} %neighbours_ref.1, f32[288,2048]{1,0:T(8,128)} %correlate_partial.1.refs_5_.before_ref, bf16[16,304,512]{2,1,0:T(8,128)(2,1)} %copy-done.2, bf16[16,32,256]{2,1,0:T(8,128)(2,1)} %copy-done.5, bf16[16,32,256]{2,1,0:T(8,128)(2,1)} %copy-done.9, ...), custom_call_target="tpu_custom_call" | custom-call | flops 4831838208 | bytes 12582912 | tf_op jit(solution)/shard_map/correlate_final/pallas_call | solution.py:257
  (50 shorter events, 2.9 us)
Async XLA Ops:
  0.7 5.3 %collective-permute-start = (bf16[48,256]{1,0:T(8,128)(2,1)S(1)}, bf16[48,256]{1,0:T(8,128)(2,1)S(1)}, u32[]{:S(2)}, u32[]{:S(2)}) collective-permute-start(bf16[48,256]{1,0:T(8,128)(2,1)S(1)} %slice.3), channel_id=1, source_target_pairs={{1,0},{2,1},{3,2},{4,3},{5,4},{6,5},{7,6},{8,7},{9,8},{10,9},{11,1... | collective-permute-start | bytes 73736 | tf_op jit(solution)/shard_map/ppermute | solution.py:27
  6.0 0.6 copy-start.15
  10.3 16.4 %copy-start.14 = (s32[64,62]{1,0:T(8,128)S(1)}, s32[64,62]{1,0:T(8,128)}, u32[]{:S(2)}) copy-start(s32[64,62]{1,0:T(8,128)} %param.7) | copy-start | bytes 47620
  10.3 16.6 %copy-start.16 = (s32[64]{0:T(128)S(1)}, s32[64]{0:T(128)}, u32[]{:S(2)}) copy-start(s32[64]{0:T(128)} %param.6) | copy-start | bytes 772
  10.3 66.6 %all-to-all-start = ((bf16[64,64,256]{2,1,0:T(8,128)(2,1)}), bf16[64,64,256]{2,1,0:T(8,128)(2,1)S(1)}, u32[]{:S(2)}, u32[]{:S(2)}) async-start(bf16[64,64,256]{2,1,0:T(8,128)(2,1)} %get-tuple-element.7), calls=%async_computation | async-start | bytes 4194304 | tf_op jit(solution)/shard_map/all_to_all | solution.py:335
  78.7 50.8 %copy-start.1 = (bf16[32,32,256]{2,1,0:T(8,128)(2,1)}, bf16[32,32,256]{2,1,0:T(8,128)(2,1)S(1)}, u32[]{:S(2)}) copy-start(bf16[32,32,256]{2,1,0:T(8,128)(2,1)S(1)} %pick_own.2.own_ref.refs_0_) | copy-start | bytes 1572868
  78.7 14.7 %collective-permute-start.1 = (bf16[32,32,256]{2,1,0:T(8,128)(2,1)S(1)}, bf16[32,32,256]{2,1,0:T(8,128)(2,1)S(1)}, u32[]{:S(2)}, u32[]{:S(2)}) collective-permute-start(bf16[32,32,256]{2,1,0:T(8,128)(2,1)S(1)} %pick_own.2.own_ref.refs_0_), channel_id=1, source_target_pairs={{0,8},{1,9},{2,10},{3,11},{4,12},{5,13},{6,14},{7,15},{8,16},{9,17... | collective-permute-start | bytes 1572872 | tf_op jit(solution)/shard_map/ppermute | solution.py:27
  93.4 5.8 %copy-start.3 = (bf16[32,32,256]{2,1,0:T(8,128)(2,1)}, bf16[32,32,256]{2,1,0:T(8,128)(2,1)S(1)}, u32[]{:S(2)}) copy-start(bf16[32,32,256]{2,1,0:T(8,128)(2,1)S(1)} %collective-permute-done.1.refs_4_.refs_1_) | copy-start | bytes 1572868
  94.6 16.3 %collective-permute-start.2 = (bf16[32,32,256]{2,1,0:T(8,128)(2,1)}, bf16[32,32,256]{2,1,0:T(8,128)(2,1)S(1)}, u32[]{:S(2)}, u32[]{:S(2)}) collective-permute-start(bf16[32,32,256]{2,1,0:T(8,128)(2,1)} %get-tuple-element.11), channel_id=1, source_target_pairs={{0,2},{1,3},{2,4},{3,5},{4,6},{5,7},{6,0},{7,1},{8,10},{9,11},{10,... | collective-permute-start | bytes 1572872 | tf_op jit(solution)/shard_map/ppermute | solution.py:33
  95.6 32.0 %collective-permute-start.3 = (bf16[32,32,256]{2,1,0:T(8,128)(2,1)}, bf16[32,32,256]{2,1,0:T(8,128)(2,1)}, u32[]{:S(2)}, u32[]{:S(2)}) collective-permute-start(bf16[32,32,256]{2,1,0:T(8,128)(2,1)} %get-tuple-element.10), channel_id=1, source_target_pairs={{0,4},{1,5},{2,6},{3,7},{4,0},{5,1},{6,2},{7,3},{8,12},{9,13},{10,... | collective-permute-start | bytes 1572872 | tf_op jit(solution)/shard_map/ppermute | solution.py:33
  98.0 31.5 %collective-permute-start.4 = (bf16[32,32,256]{2,1,0:T(8,128)(2,1)S(1)}, bf16[32,32,256]{2,1,0:T(8,128)(2,1)}, u32[]{:S(2)}, u32[]{:S(2)}) collective-permute-start(bf16[32,32,256]{2,1,0:T(8,128)(2,1)S(1)} %get-tuple-element.9), channel_id=1, source_target_pairs={{0,6},{1,7},{2,0},{3,1},{4,2},{5,3},{6,4},{7,5},{8,14},{9,15},{10,... | collective-permute-start | bytes 1572872 | tf_op jit(solution)/shard_map/ppermute | solution.py:33
  99.2 36.9 %all-to-all-start.1 = ((bf16[64,32,256]{2,1,0:T(8,128)(2,1)}), bf16[64,32,256]{2,1,0:T(8,128)(2,1)S(1)}, u32[]{:S(2)}, u32[]{:S(2)}) async-start(bf16[64,32,256]{2,1,0:T(8,128)(2,1)} %hold.1), calls=%async_computation.1 | async-start | bytes 2097152 | tf_op jit(solution)/shard_map/all_to_all | solution.py:335
  107.6 21.9 %copy-start.4 = (bf16[32,32,256]{2,1,0:T(8,128)(2,1)S(1)}, bf16[32,32,256]{2,1,0:T(8,128)(2,1)}, u32[]{:S(2)}) copy-start(bf16[32,32,256]{2,1,0:T(8,128)(2,1)} %copy-done.3) | copy-start | bytes 1572868
  110.9 21.1 %copy-start = (bf16[32,304,512]{2,1,0:T(8,128)(2,1)}, bf16[32,304,512]{2,1,0:T(8,128)(2,1)S(1)}, u32[]{:S(2)}) copy-start(bf16[32,304,512]{2,1,0:T(8,128)(2,1)S(1)} %shifted.2.refs_5_.q_ref) | copy-start | bytes 29884420
  110.9 21.0 %copy-start.8 = (bf16[32,32,256]{2,1,0:T(8,128)(2,1)}, bf16[32,32,256]{2,1,0:T(8,128)(2,1)S(1)}, u32[]{:S(2)}) copy-start(bf16[32,32,256]{2,1,0:T(8,128)(2,1)S(1)} %collective-permute-done.2.refs_1_) | copy-start | bytes 1572868
  132.0 18.6 %collective-permute-start.5 = (bf16[4,32,32,256]{3,2,1,0:T(8,128)(2,1)}, bf16[4,32,32,256]{3,2,1,0:T(8,128)(2,1)}, u32[]{:S(2)}, u32[]{:S(2)}) collective-permute-start(bf16[4,32,32,256]{3,2,1,0:T(8,128)(2,1)} %exchange.2), channel_id=1, source_target_pairs={{0,1},{1,0},{2,3},{3,2},{4,5},{5,4},{6,7},{7,6},{8,9},{9,8},{10,11... | collective-permute-start | bytes 6291464 | tf_op jit(solution)/shard_map/ppermute | solution.py:37
  137.3 28.2 %copy-start.5 = (bf16[16,32,256]{2,1,0:T(8,128)(2,1)}, bf16[16,32,256]{2,1,0:T(8,128)(2,1)S(1)}, u32[]{:S(2)}) copy-start(bf16[16,32,256]{2,1,0:T(8,128)(2,1)S(1)} %pick_own.3.own_ref.refs_0_) | copy-start | bytes 786436
  137.3 9.8 %collective-permute-start.6 = (bf16[16,32,256]{2,1,0:T(8,128)(2,1)S(1)}, bf16[16,32,256]{2,1,0:T(8,128)(2,1)S(1)}, u32[]{:S(2)}, u32[]{:S(2)}) collective-permute-start(bf16[16,32,256]{2,1,0:T(8,128)(2,1)S(1)} %pick_own.3.own_ref.refs_0_), channel_id=1, source_target_pairs={{0,8},{1,9},{2,10},{3,11},{4,12},{5,13},{6,14},{7,15},{8,16},{9,17... | collective-permute-start | bytes 786440 | tf_op jit(solution)/shard_map/ppermute | solution.py:27
  140.9 2.3 %copy-start.2 = (bf16[16,304,512]{2,1,0:T(8,128)(2,1)}, bf16[16,304,512]{2,1,0:T(8,128)(2,1)S(1)}, u32[]{:S(2)}) copy-start(bf16[16,304,512]{2,1,0:T(8,128)(2,1)S(1)} %shifted.3.refs_9_.q_ref) | copy-start | bytes 14942212
  147.1 18.4 %copy-start.7 = (bf16[16,32,256]{2,1,0:T(8,128)(2,1)}, bf16[16,32,256]{2,1,0:T(8,128)(2,1)S(1)}, u32[]{:S(2)}) copy-start(bf16[16,32,256]{2,1,0:T(8,128)(2,1)S(1)} %collective-permute-done.6.refs_4_) | copy-start | bytes 786436
  147.9 2.7 %copy-start.12 = (bf16[16,32,256]{2,1,0:T(8,128)(2,1)}, bf16[16,32,256]{2,1,0:T(8,128)(2,1)S(1)}, u32[]{:S(2)}) copy-start(bf16[16,32,256]{2,1,0:T(8,128)(2,1)S(1)} %get-tuple-element.12.refs_8_) | copy-start | bytes 786436
  147.9 2.7 %copy-start.13 = (bf16[16,32,256]{2,1,0:T(8,128)(2,1)}, bf16[16,32,256]{2,1,0:T(8,128)(2,1)S(1)}, u32[]{:S(2)}) copy-start(bf16[16,32,256]{2,1,0:T(8,128)(2,1)S(1)} %get-tuple-element.13.refs_7_) | copy-start | bytes 786436
  147.9 17.5 %collective-permute-start.7 = (bf16[16,32,256]{2,1,0:T(8,128)(2,1)}, bf16[16,32,256]{2,1,0:T(8,128)(2,1)S(1)}, u32[]{:S(2)}, u32[]{:S(2)}) collective-permute-start(bf16[16,32,256]{2,1,0:T(8,128)(2,1)} %get-tuple-element.14.refs_6_), channel_id=1, source_target_pairs={{0,2},{1,3},{2,4},{3,5},{4,6},{5,7},{6,0},{7,1},{8,10},{9,11},{10,... | collective-permute-start | bytes 786440 | tf_op jit(solution)/shard_map/ppermute | solution.py:33
  147.9 17.5 %collective-permute-start.8 = (bf16[16,32,256]{2,1,0:T(8,128)(2,1)S(1)}, bf16[16,32,256]{2,1,0:T(8,128)(2,1)S(1)}, u32[]{:S(2)}, u32[]{:S(2)}) collective-permute-start(bf16[16,32,256]{2,1,0:T(8,128)(2,1)S(1)} %get-tuple-element.13.refs_7_), channel_id=1, source_target_pairs={{0,4},{1,5},{2,6},{3,7},{4,0},{5,1},{6,2},{7,3},{8,12},{9,13},{10,... | collective-permute-start | bytes 786440 | tf_op jit(solution)/shard_map/ppermute | solution.py:33
  149.7 15.7 %collective-permute-start.9 = (bf16[16,32,256]{2,1,0:T(8,128)(2,1)S(1)}, bf16[16,32,256]{2,1,0:T(8,128)(2,1)S(1)}, u32[]{:S(2)}, u32[]{:S(2)}) collective-permute-start(bf16[16,32,256]{2,1,0:T(8,128)(2,1)S(1)} %get-tuple-element.12.refs_8_), channel_id=1, source_target_pairs={{0,6},{1,7},{2,0},{3,1},{4,2},{5,3},{6,4},{7,5},{8,14},{9,15},{10,... | collective-permute-start | bytes 786440 | tf_op jit(solution)/shard_map/ppermute | solution.py:33
  165.4 2.1 %copy-start.9 = (bf16[16,32,256]{2,1,0:T(8,128)(2,1)}, bf16[16,32,256]{2,1,0:T(8,128)(2,1)S(1)}, u32[]{:S(2)}) copy-start(bf16[16,32,256]{2,1,0:T(8,128)(2,1)S(1)} %collective-permute-done.7.refs_1_) | copy-start | bytes 786436
  165.4 2.1 %copy-start.10 = (bf16[16,32,256]{2,1,0:T(8,128)(2,1)}, bf16[16,32,256]{2,1,0:T(8,128)(2,1)S(1)}, u32[]{:S(2)}) copy-start(bf16[16,32,256]{2,1,0:T(8,128)(2,1)S(1)} %collective-permute-done.8.refs_2_) | copy-start | bytes 786436
  165.5 1.8 copy-start.6
  167.3 0.7 copy-start.11
  168.0 4.9 %collective-permute-start.10 = (bf16[4,16,32,256]{3,2,1,0:T(8,128)(2,1)S(1)}, bf16[4,16,32,256]{3,2,1,0:T(8,128)(2,1)}, u32[]{:S(2)}, u32[]{:S(2)}) collective-permute-start(bf16[4,16,32,256]{3,2,1,0:T(8,128)(2,1)S(1)} %exchange.3), channel_id=1, source_target_pairs={{0,1},{1,0},{2,3},{3,2},{4,5},{5,4},{6,7},{7,6},{8,9},{9,8},{10,11... | collective-permute-start | bytes 3145736 | tf_op jit(solution)/shard_map/ppermute | solution.py:37

commit v2 on v1

v2 whole, which is shorter than its diff:
```python
import functools

import jax
import jax.numpy as jnp
from jax import lax
from jax.experimental import pallas as pl
from jax.experimental.pallas import tpu as pltpu
from jax.sharding import PartitionSpec as P

WIN = 256
MAXLAG = 30
LAGS = 2 * MAXLAG + 1
SHIFTS = 16
STEPS = 4
Q_ROWS = WIN + SHIFTS * (STEPS - 1)
LANE = 128
VMEM_LIMIT = 24 * 2**20
LITTLE = pl.CostEstimate(flops=1, bytes_accessed=1, transcendentals=0)
TOKEN = jax.ShapeDtypeStruct((8, LANE), jnp.float32)
CHUNKS = (24, 24)


ROW = 4


def from_behind(array, axis, by):
    devices = lax.axis_size(axis)
    pairs = [(i, i + by) for i in range(devices) if 0 <= i + by < devices]
    return lax.ppermute(array, axis, pairs)


def along_row(array, by):
    row = 2 * ROW
    devices = lax.axis_size("ev")
    return lax.ppermute(array, "ev", [(i, i // row * row + (i % row + 2 * by) % row) for i in range(devices)])


def between_cores(array):
    return lax.ppermute(array, "ev", [(i, i ^ 1) for i in range(lax.axis_size("ev"))])


def cut_kernel(offset_ref, owner_ref, count_ref, traces_ref, rim_ref, bucket_ref, ext_ref):
    components, segment = traces_ref.shape
    ext_ref[:, :segment] = traces_ref[...]
    ext_ref[:, segment:] = rim_ref[...]

    def cut_pair(pair, carry):
        owner = owner_ref[2 * pair]
        for which in range(2):
            offset = offset_ref[2 * pair + which]
            base = pl.multiple_of(offset // LANE * LANE, LANE)
            rest = offset - base
            span = ext_ref[:, pl.ds(base, WIN + LANE)].astype(jnp.float32)
            span = pltpu.roll(span, WIN + LANE - rest, axis=1)
            bucket_ref[owner, which * components : (which + 1) * components, :] = span[:, :WIN].astype(
                jnp.bfloat16
            )
        return carry

    lax.fori_loop(0, count_ref[0] // 2, cut_pair, 0)


def cut_windows(offset, owner, count, traces, rim, devices):
    components, segment = traces.shape
    return pl.pallas_call(
        cut_kernel,
        out_shape=jax.ShapeDtypeStruct((devices, 2 * components, WIN), jnp.bfloat16),
        in_specs=[pl.BlockSpec(memory_space=pltpu.SMEM)] * 3 + [pl.BlockSpec(memory_space=pltpu.VMEM)] * 2,
        out_specs=pl.BlockSpec(memory_space=pltpu.VMEM),
        scratch_shapes=[pltpu.VMEM((components, segment + WIN), jnp.bfloat16)],
        cost_estimate=LITTLE,
        compiler_params=pltpu.CompilerParams(vmem_limit_bytes=60 * 2**20),
        name="cut_windows",
    )(offset, owner, count, traces, rim)


def pick_kernel(source_ref, arrived_ref, *refs):
    own_refs, rows_ref = refs[:-1], refs[-1]
    components = arrived_ref.shape[1] // 2
    events = own_refs[0].shape[1]
    for event in range(events):
        source = source_ref[event]
        half = pl.multiple_of(source % 2 * components, 16)
        window = arrived_ref[source // 2, pl.ds(half, components), :].astype(jnp.float32)
        for part in range(WIN // LANE):
            rows_ref[part, pl.ds(event, components, stride=events), :] = window[:, part * LANE : (part + 1) * LANE]
    component = 0
    for own_ref in own_refs:
        for place in range(own_ref.shape[0]):
            for part in range(WIN // LANE):
                own_ref[place, :, part * LANE : (part + 1) * LANE] = rows_ref[
                    part, component * events : (component + 1) * events, :
                ].astype(jnp.bfloat16)
            component += 1


def pick_own(source, arrived, events):
    components = arrived.shape[1] // 2
    return pl.pallas_call(
        pick_kernel,
        out_shape=[jax.ShapeDtypeStruct((size, events, WIN), jnp.bfloat16) for size in CHUNKS],
        in_specs=[pl.BlockSpec(memory_space=pltpu.SMEM), pl.BlockSpec(memory_space=pltpu.VMEM)],
        out_specs=[pl.BlockSpec(memory_space=pltpu.VMEM)] * len(CHUNKS),
        scratch_shapes=[pltpu.VMEM((WIN // LANE, components * events, LANE), jnp.float32)],
        cost_estimate=LITTLE,
        compiler_params=pltpu.CompilerParams(vmem_limit_bytes=VMEM_LIMIT),
        name="pick_own",
    )(source, arrived)


def shift_kernel(own_ref, q_ref, token_ref, padded_ref, quad_ref):
    token_ref[...] = jnp.zeros_like(token_ref)
    per_lane = LANE // own_ref.shape[1]
    margin = 40
    quads = quad_ref.shape[0]
    block = lax.broadcasted_iota(jnp.int32, (1, LANE), 1) // own_ref.shape[1]
    padded_ref[:margin, :] = jnp.zeros((margin, LANE), jnp.float32)
    tail = padded_ref.shape[0] - margin - WIN
    padded_ref[margin + WIN :, :] = jnp.zeros((tail, LANE), jnp.float32)
    for step in range(own_ref.shape[0]):
        window = own_ref[step].astype(jnp.float32)
        window = jnp.concatenate([window] * per_lane, axis=0)
        for part in range(WIN // LANE):
            padded_ref[margin + part * LANE : margin + (part + 1) * LANE, :] = window[
                :, part * LANE : (part + 1) * LANE
            ].T
        first = margin - 16 - 18
        quad = padded_ref[first : first + quads, :]
        for shift in range(1, per_lane):
            quad = jnp.where(block == shift, padded_ref[first - shift : first - shift + quads, :], quad)
        quad_ref[...] = quad
        for group in range(SHIFTS // per_lane):
            begin = 16 - per_lane * group
            q_ref[step, :, group * LANE : (group + 1) * LANE] = quad_ref[begin : begin + Q_ROWS, :].astype(
                jnp.bfloat16
            )


def shifted(own, batch=4):
    components, events, _ = own.shape
    width = SHIFTS * events
    return pl.pallas_call(
        shift_kernel,
        out_shape=[jax.ShapeDtypeStruct((components, Q_ROWS, width), jnp.bfloat16), TOKEN],
        grid=(components // batch,),
        in_specs=[pl.BlockSpec((batch, events, WIN), lambda c: (c, 0, 0))],
        out_specs=[
            pl.BlockSpec((batch, Q_ROWS, width), lambda c: (c, 0, 0)),
            pl.BlockSpec(TOKEN.shape, lambda c: (0, 0)),
        ],
        scratch_shapes=[pltpu.VMEM((328, LANE), jnp.float32), pltpu.VMEM((320, LANE), jnp.float32)],
        cost_estimate=LITTLE,
        compiler_params=pltpu.CompilerParams(vmem_limit_bytes=VMEM_LIMIT),
        name="shifted",
    )(own)


def accumulate(q_ref, pieces, band_ref, acc_ref):
    batch, events, _ = pieces[0].shape
    width = q_ref.shape[2]
    same, other = pieces[:-1], pieces[-1]
    for c in range(batch):
        for k in range(len(same)):
            band_ref[2 * k * events : (2 * k + 1) * events, :] = same[k][c]
        for k in range(other.shape[0]):
            band_ref[(2 * k + 1) * events : (2 * k + 2) * events, :] = other[k, c]
        band = band_ref[...].astype(jnp.float32)
        row_norm = lax.rsqrt(jnp.sum(band * band, axis=1, keepdims=True) + 1e-06)
        own = q_ref[c, :, :LANE].astype(jnp.float32)
        lane_norm = lax.rsqrt(jnp.sum(own * own, axis=0, keepdims=True) + 1e-06)
        weight = row_norm * lane_norm
        weight = jnp.concatenate([weight, weight], axis=1)
        for m in range(STEPS):
            begin = SHIFTS * (STEPS - 1 - m)
            for half in range(width // 256):
                products = jnp.dot(
                    band_ref[...],
                    q_ref[c, begin : begin + WIN, half * 256 : (half + 1) * 256],
                    preferred_element_type=jnp.float32,
                )
                place = m * width + half * 256
                acc_ref[:, place : place + 256] += products * weight


def partial_kernel(started, count, q_ref, *refs):
    acc_ref, token_ref, band_ref = refs[-3:]

    @pl.when(pl.program_id(0) == 0)
    def _():
        token_ref[...] = jnp.zeros_like(token_ref)
        acc_ref[...] = refs[0][...] if started else jnp.zeros_like(acc_ref)

    accumulate(q_ref, refs[started : started + count], band_ref, acc_ref)


def final_kernel(neighbours_ref, before_ref, q_ref, *refs):
    pieces, (out_ref, band_ref, acc_ref, turned_ref, spread_ref) = refs[:-5], refs[-5:]
    events = pieces[0].shape[1]
    rows = band_ref.shape[0]
    step = pl.program_id(0)

    @pl.when(step == 0)
    def _():
        acc_ref[...] = before_ref[...]

    accumulate(q_ref, pieces, band_ref, acc_ref)

    @pl.when(step == pl.num_programs(0) - 1)
    def _():
        for column in range(acc_ref.shape[1] // LANE):
            for tile in range(turned_ref.shape[0]):
                first, last = tile * LANE, min((tile + 1) * LANE, rows)
                turned_ref[tile, column * LANE : (column + 1) * LANE, : last - first] = acc_ref[
                    first:last, column * LANE : (column + 1) * LANE
                ].T
        lags = STEPS * SHIFTS
        row = lax.broadcasted_iota(jnp.int32, (rows, neighbours_ref.shape[1]), 0)
        for event in range(events):
            sums = jnp.concatenate(
                [turned_ref[tile, pl.ds(event, lags, stride=events), :] for tile in range(turned_ref.shape[0])], axis=1
            )[:, :rows]
            high = sums.astype(jnp.bfloat16)
            low = (sums - high.astype(jnp.float32)).astype(jnp.bfloat16)
            chosen = (row == neighbours_ref[event : event + 1, :]).astype(jnp.bfloat16)
            both = jnp.dot(jnp.concatenate([high, low], axis=0), chosen, preferred_element_type=jnp.float32)
            total = both[:lags] + both[lags:]
            spread_ref[pl.ds(event, lags, stride=events), :] = total
        out_ref[...] = spread_ref[: LAGS * events]


def piece_specs(pieces, batch):
    same, other = pieces[:-1], pieces[-1]
    return [pl.BlockSpec((batch, *x.shape[1:]), lambda c: (c, 0, 0)) for x in same] + [
        pl.BlockSpec((other.shape[0], batch, *other.shape[2:]), lambda c: (0, c, 0, 0))
    ]


def correlate_partial(before, q, pieces, after, batch=4):
    components, events, _ = pieces[0].shape
    rows = (len(pieces) - 1 + pieces[-1].shape[0]) * events
    width = q.shape[2]
    sums = pl.BlockSpec((rows, STEPS * width), lambda c: (0, 0))
    return pl.pallas_call(
        functools.partial(partial_kernel, len(before), len(pieces)),
        out_shape=[jax.ShapeDtypeStruct((rows, STEPS * width), jnp.float32), TOKEN],
        grid=(components // batch,),
        in_specs=[pl.BlockSpec((batch, Q_ROWS, width), lambda c: (c, 0, 0))]
        + [sums] * len(before)
        + piece_specs(pieces, batch)
        + [pl.BlockSpec(memory_space=pl.ANY)] * len(after),
        out_specs=[sums, pl.BlockSpec(TOKEN.shape, lambda c: (0, 0))],
        scratch_shapes=[pltpu.VMEM((rows, WIN), jnp.bfloat16)],
        cost_estimate=LITTLE,
        compiler_params=pltpu.CompilerParams(vmem_limit_bytes=VMEM_LIMIT),
        name="correlate_partial",
    )(q, *before, *pieces, *after)


def correlate_final(neighbours, before, q, pieces, batch=4):
    components, events, _ = pieces[0].shape
    rows = (len(pieces) - 1 + pieces[-1].shape[0]) * events
    width = q.shape[2]
    k = neighbours.shape[1]
    tiles = (rows + LANE - 1) // LANE
    sums = pl.pallas_call(
        final_kernel,
        out_shape=jax.ShapeDtypeStruct((LAGS * events, k), jnp.float32),
        grid=(components // batch,),
        in_specs=[
            pl.BlockSpec((events, k), lambda c: (0, 0)),
            pl.BlockSpec((rows, STEPS * width), lambda c: (0, 0)),
            pl.BlockSpec((batch, Q_ROWS, width), lambda c: (c, 0, 0)),
        ]
        + piece_specs(pieces, batch),
        out_specs=pl.BlockSpec((LAGS * events, k), lambda c: (0, 0)),
        scratch_shapes=[
            pltpu.VMEM((rows, WIN), jnp.bfloat16),
            pltpu.VMEM((rows, STEPS * width), jnp.float32),
            pltpu.VMEM((tiles, STEPS * width, LANE), jnp.float32),
            pltpu.VMEM((STEPS * width, k), jnp.float32),
        ],
        cost_estimate=LITTLE,
        compiler_params=pltpu.CompilerParams(vmem_limit_bytes=VMEM_LIMIT),
        name="correlate_final",
    )(neighbours, before, q, *pieces)
    return jnp.transpose(sums.reshape(LAGS, events, k), (1, 0, 2))


def exchange_kernel(count, core_ref, *refs):
    blocks, sent_ref = refs[:count], refs[-1]
    for core in range(2):

        @pl.when(core_ref[0] == core)
        def _(core=core):
            for k in range(count - 1):
                sent_ref[k] = blocks[k + core][...]


def exchange(core, blocks, after):
    sent = pl.pallas_call(
        functools.partial(exchange_kernel, len(blocks)),
        out_shape=jax.ShapeDtypeStruct((len(blocks) - 1, *blocks[0].shape), blocks[0].dtype),
        in_specs=[pl.BlockSpec(memory_space=pltpu.SMEM)]
        + [pl.BlockSpec(memory_space=pltpu.VMEM)] * len(blocks)
        + [pl.BlockSpec(memory_space=pl.ANY)] * len(after),
        out_specs=pl.BlockSpec(memory_space=pltpu.VMEM),
        cost_estimate=LITTLE,
        compiler_params=pltpu.CompilerParams(vmem_limit_bytes=VMEM_LIMIT),
        name="exchange",
    )(core, *blocks, *after)
    return between_cores(sent)


def row_kernel(y_ref, own_ref, above_ref, *refs):
    sent, token_ref = refs[-ROW:-1], refs[-1]
    for by in range(1, ROW):

        @pl.when(y_ref[0] + by >= ROW)
        def _(by=by):
            sent[by - 1][...] = above_ref[...]

        @pl.when(y_ref[0] + by < ROW)
        def _(by=by):
            sent[by - 1][...] = own_ref[...]

    token_ref[...] = jnp.zeros_like(token_ref)


def along_rows(y, own, above, after):
    *sent, token = pl.pallas_call(
        row_kernel,
        out_shape=[jax.ShapeDtypeStruct(own.shape, own.dtype)] * (ROW - 1) + [TOKEN],
        in_specs=[pl.BlockSpec(memory_space=pltpu.SMEM)]
        + [pl.BlockSpec(memory_space=pltpu.VMEM)] * 2
        + [pl.BlockSpec(memory_space=pl.ANY)] * len(after),
        out_specs=[pl.BlockSpec(memory_space=pltpu.VMEM)] * ROW,
        cost_estimate=LITTLE,
        compiler_params=pltpu.CompilerParams(vmem_limit_bytes=VMEM_LIMIT),
        name="along_rows",
    )(y, own, above, *after)
    return [along_row(x, by) for by, x in enumerate(sent, 1)], token


def body(traces, held_count, window_owner_table, pick_offset, neighbours):
    devices = lax.axis_size("ev")
    own_index = lax.axis_index("ev")
    held_slots = window_owner_table.shape[1]
    per_dev = neighbours.shape[0]
    next_rim = from_behind(traces[:, :WIN], "ev", -1)

    my_row = lax.dynamic_index_in_dim(window_owner_table, own_index, 0, keepdims=False)
    held_here = lax.dynamic_index_in_dim(held_count, own_index, 0, keepdims=True)
    bucket = cut_windows(pick_offset[0], my_row // per_dev, held_here, traces, next_rim, devices)
    arrived = lax.all_to_all(bucket, "ev", split_axis=0, concat_axis=0, tiled=True)

    slots = jnp.arange(held_slots, dtype=jnp.int32)
    all_live = slots[None, :] < held_count[:, None]
    wanted = own_index * per_dev + jnp.arange(per_dev, dtype=jnp.int32)
    matches = all_live[None] & (window_owner_table[None] == wanted[:, None, None])
    place = 2 * jnp.arange(devices, dtype=jnp.int32)[:, None] + slots[None, :] % 2
    source = jnp.sum(jnp.where(matches, place[None], 0), axis=(1, 2))

    y, core = (own_index // 2 % ROW)[None], (own_index % 2)[None]

    owns = pick_own(source, arrived, per_dev)
    aboves = [from_behind(own, "ev", 2 * ROW) for own in owns]
    shifts = [shifted(own) for own in owns]
    rows, sent = [], []
    for index, (own, above) in enumerate(zip(owns, aboves)):
        row, token = along_rows(y, own, above, [shifts[index][1]])
        rows.append(row)
        sent.append(token)
    last = len(owns) - 1
    sums, summed = [], []
    for index in range(last + 1):
        blocks = [owns[index], *rows[index], aboves[index]]
        pieces = blocks + [exchange(core, blocks, summed + [sent[min(index + 1, last)]])]
        if index == last:
            return correlate_final(neighbours, *sums, shifts[index][0], pieces)
        total, token = correlate_partial(sums, shifts[index][0], pieces, [sent[min(index + 2, last)]])
        sums, summed = [total], [token]


def solution(mesh):
    in_specs = (
        P("sta", "ev"),
        P("sta"),
        P("sta", None),
        P(("sta", "ev"), None),
        P(("sta", "ev"), None),
    )
    out_specs = P(("sta", "ev"), None, None)
    return jax.shard_map(body, mesh=mesh, in_specs=in_specs, out_specs=out_specs, check_vma=False)
```

time: 187 us -> 181 us (0.968)
  the two profiles are of different devices: /device:TPU:35 before, /device:TPU:57 now
where the time goes in v2:
time: 181 us; the launch traced here: 179 us
  waiting for transfers between devices  97.9 us (54%)
  Pallas kernels  42.8 us (24%)
  starting transfers between devices  24.1 us (13%)
  local copies, waits for them, and re-layouts  11.7 us (6%)
  other arithmetic  1.84 us (1%)
    all_to_all x1, waiting for transfers between devices, body(): lax.all_to_all(bucket, 'ev', split_axis=0, concat_axis=0, tiled=True)  72 us
    ppermute x6, waiting for transfers between devices, along_row(): lax.ppermute(array, 'ev', [(i, i // row * row + (i % row + 2 * by) % row)...  16.8 us
    pallas_call x1, Pallas kernels, correlate_final(): pl.pallas_call(final_kernel, out_shape=jax.ShapeDtypeStruct((LAGS * event...  14.1 us
    all_to_all x1, starting transfers between devices, body(): lax.all_to_all(bucket, 'ev', split_axis=0, concat_axis=0, tiled=True)  11.3 us
    pallas_call x1, Pallas kernels, correlate_partial(): pl.pallas_call(functools.partial(partial_kernel, len(before), len(pieces)...  9.77 us
    unnamed x25, local copies, waits for them, and re-layouts  9.76 us
    pallas_call x2, Pallas kernels, shifted(): pl.pallas_call(shift_kernel, out_shape=[jax.ShapeDtypeStruct((components,...  6.61 us
    ppermute x3, starting transfers between devices, from_behind(): return lax.ppermute(array, axis, pairs)  6.39 us
  transfers between devices with their start and end apart: 12, of which 10 were waited for; matrix products, arithmetic and copies ran while one was open for 2% of the time, Pallas kernels for 10%

profile of v2, /device:TPU:57, one launch (start us, length us, event | category | flops | bytes accessed | tf_op | source)
XLA Modules:
  0.0 178.6 jit_solution(5977068351817915468)
XLA Ops:
  0.7 2.6 %collective-permute-start = (bf16[48,256]{1,0:T(8,128)(2,1)S(1)}, bf16[48,256]{1,0:T(8,128)(2,1)S(1)}, u32[]{:S(2)}, u32[]{:S(2)}) collective-permute-start(bf16[48,256]{1,0:T(8,128)(2,1)S(1)} %slice.3), channel_id=1, source_target_pairs={{1,0},{2,1},{3,2},{4,3},{5,4},{6,5},{7,6},{8,7},{9,8},{10,9},{11,1... | collective-permute-start | bytes 73736 | tf_op jit(solution)/shard_map/ppermute | solution.py:29
  3.3 1.3 and_select_fusion.owner_ref
  4.6 1.2 dynamic_slice.9.count_ref
  5.8 2.1 %collective-permute-done.rim_ref = bf16[48,256]{1,0:T(8,128)(2,1)S(1)} collective-permute-done((bf16[48,256]{1,0:T(8,128)(2,1)S(1)}, bf16[48,256]{1,0:T(8,128)(2,1)S(1)}, u32[]{:S(2)}, u32[]{:S(2)}) %collective-permute-start) | collective-permute-done | bytes 24608 | tf_op jit(solution)/shard_map/ppermute | solution.py:29
  8.6 6.1 %cut_windows.1 = bf16[64,96,256]{2,1,0:T(8,128)(2,1)} custom-call(s32[62]{0:T(128)} %bitcast.14, s32[62]{0:T(128)} %and_select_fusion.owner_ref, s32[1]{0:T(128)} %dynamic_slice.9.count_ref, bf16[48,8192]{1,0:T(8,128)(2,1)} %traces_ref.1, bf16[48,256]{1,0:T(8,128)(2,1)} %copy-done.10), custom_call_target="tpu_custom_call" | custom-call | flops 1 | bytes 1 | tf_op jit(solution)/shard_map/cut_windows/pallas_call | solution.py:65
  14.7 11.3 %all-to-all-start = ((bf16[64,96,256]{2,1,0:T(8,128)(2,1)}), bf16[64,96,256]{2,1,0:T(8,128)(2,1)S(1)}, u32[]{:S(2)}, u32[]{:S(2)}) async-start(bf16[64,96,256]{2,1,0:T(8,128)(2,1)} %cut_windows.1), calls=%async_computation | async-start | bytes 6291456 | tf_op jit(solution)/shard_map/all_to_all | solution.py:354
  26.7 72.0 %all-to-all-done.arrived_ref = bf16[64,96,256]{2,1,0:T(8,128)(2,1)S(1)} async-done(((bf16[64,96,256]{2,1,0:T(8,128)(2,1)}), bf16[64,96,256]{2,1,0:T(8,128)(2,1)S(1)}, u32[]{:S(2)}, u32[]{:S(2)}) %all-to-all-start) | async-done | bytes 3145760 | tf_op jit(solution)/shard_map/all_to_all | solution.py:354
  98.7 3.0 %pick_own.1 = (bf16[24,32,256]{2,1,0:T(8,128)(2,1)}, bf16[24,32,256]{2,1,0:T(8,128)(2,1)S(1)}) custom-call(s32[32]{0:T(128)S(1)} %select_reduce_fusion.source_ref, bf16[64,96,256]{2,1,0:T(8,128)(2,1)S(1)} %all-to-all-done.arrived_ref), custom_call_target="tpu_custom_call" | custom-call | flops 1 | bytes 1 | tf_op jit(solution)/shard_map/pick_own/pallas_call | solution.py:99
  101.8 1.9 %collective-permute-start.1 = (bf16[24,32,256]{2,1,0:T(8,128)(2,1)}, bf16[24,32,256]{2,1,0:T(8,128)(2,1)S(1)}, u32[]{:S(2)}, u32[]{:S(2)}) collective-permute-start(bf16[24,32,256]{2,1,0:T(8,128)(2,1)} %get-tuple-element.20.own_ref.refs_0_), channel_id=1, source_target_pairs={{0,8},{1,9},{2,10},{3,11},{4,12},{5,13},{6,14},{7,15},{8,16},{9,17... | collective-permute-start | bytes 1179656 | tf_op jit(solution)/shard_map/ppermute | solution.py:29
  103.7 4.2 %shifted.2 = (bf16[24,304,512]{2,1,0:T(8,128)(2,1)S(1)}, f32[8,128]{1,0:T(8,128)S(1)}) custom-call(bf16[24,32,256]{2,1,0:T(8,128)(2,1)} %get-tuple-element.20.own_ref.refs_0_), custom_call_target="tpu_custom_call" | custom-call | flops 1 | bytes 1 | tf_op jit(solution)/shard_map/shifted/pallas_call | solution.py:142
  107.9 2.9 %copy-done = bf16[24,304,512]{2,1,0:T(8,128)(2,1)} copy-done((bf16[24,304,512]{2,1,0:T(8,128)(2,1)}, bf16[24,304,512]{2,1,0:T(8,128)(2,1)S(1)}, u32[]{:S(2)}) %copy-start) | copy-done | bytes 7471128
  110.8 1.9 %collective-permute-start.5 = (bf16[24,32,256]{2,1,0:T(8,128)(2,1)S(1)}, bf16[24,32,256]{2,1,0:T(8,128)(2,1)S(1)}, u32[]{:S(2)}, u32[]{:S(2)}) collective-permute-start(bf16[24,32,256]{2,1,0:T(8,128)(2,1)S(1)} %get-tuple-element.26.own_ref.refs_0_), channel_id=1, source_target_pairs={{0,8},{1,9},{2,10},{3,11},{4,12},{5,13},{6,14},{7,15},{8,16},{9,17... | collective-permute-start | bytes 1179656 | tf_op jit(solution)/shard_map/ppermute | solution.py:29
  112.7 1.2 collective-permute-done.1.above_ref.refs_4_
  114.0 1.7 along_rows.2
  115.7 2.3 %collective-permute-start.3 = (bf16[24,32,256]{2,1,0:T(8,128)(2,1)S(1)}, bf16[24,32,256]{2,1,0:T(8,128)(2,1)S(1)}, u32[]{:S(2)}, u32[]{:S(2)}) collective-permute-start(bf16[24,32,256]{2,1,0:T(8,128)(2,1)S(1)} %get-tuple-element.24), channel_id=1, source_target_pairs={{0,4},{1,5},{2,6},{3,7},{4,0},{5,1},{6,2},{7,3},{8,12},{9,13},{10,... | collective-permute-start | bytes 1179656 | tf_op jit(solution)/shard_map/ppermute | solution.py:35
  118.0 2.4 %shifted.3 = (bf16[24,304,512]{2,1,0:T(8,128)(2,1)S(1)}, f32[8,128]{1,0:T(8,128)S(1)}) custom-call(bf16[24,32,256]{2,1,0:T(8,128)(2,1)S(1)} %get-tuple-element.26.own_ref.refs_0_), custom_call_target="tpu_custom_call" | custom-call | flops 1 | bytes 1 | tf_op jit(solution)/shard_map/shifted/pallas_call | solution.py:142
  120.5 2.3 %collective-permute-done.5.above_ref.refs_4_ = bf16[24,32,256]{2,1,0:T(8,128)(2,1)S(1)} collective-permute-done((bf16[24,32,256]{2,1,0:T(8,128)(2,1)S(1)}, bf16[24,32,256]{2,1,0:T(8,128)(2,1)S(1)}, u32[]{:S(2)}, u32[]{:S(2)}) %collective-permute-start.5) | collective-permute-done | bytes 393248 | tf_op jit(solution)/shard_map/ppermute | solution.py:29
  122.9 2.0 %collective-permute-done.2.refs_1_ = bf16[24,32,256]{2,1,0:T(8,128)(2,1)S(1)} collective-permute-done((bf16[24,32,256]{2,1,0:T(8,128)(2,1)S(1)}, bf16[24,32,256]{2,1,0:T(8,128)(2,1)S(1)}, u32[]{:S(2)}, u32[]{:S(2)}) %collective-permute-start.2) | collective-permute-done | bytes 393248 | tf_op jit(solution)/shard_map/ppermute | solution.py:35
  124.9 1.2 collective-permute-done.3.refs_2_
  126.1 10.6 %collective-permute-done.4.refs_3_ = bf16[24,32,256]{2,1,0:T(8,128)(2,1)S(1)} collective-permute-done((bf16[24,32,256]{2,1,0:T(8,128)(2,1)S(1)}, bf16[24,32,256]{2,1,0:T(8,128)(2,1)S(1)}, u32[]{:S(2)}, u32[]{:S(2)}) %collective-permute-start.4) | collective-permute-done | bytes 393248 | tf_op jit(solution)/shard_map/ppermute | solution.py:35
  136.6 1.2 exchange.2
  138.5 1.0 collective-permute-start.7
  139.5 1.6 collective-permute-start.8
  141.5 3.1 %copy-done.1 = bf16[24,304,512]{2,1,0:T(8,128)(2,1)S(1)} copy-done((bf16[24,304,512]{2,1,0:T(8,128)(2,1)S(1)}, bf16[24,304,512]{2,1,0:T(8,128)(2,1)}, u32[]{:S(2)}) %copy-start.1) | copy-done | bytes 7471128
  144.6 1.0 copy-done.3
  145.6 1.0 copy-done.5
  146.6 1.0 copy-done.7
  147.6 9.8 %correlate_partial.1 = (f32[288,2048]{1,0:T(8,128)S(1)}, f32[8,128]{1,0:T(8,128)S(1)}) custom-call(bf16[24,304,512]{2,1,0:T(8,128)(2,1)S(1)} %copy-done.1, bf16[24,32,256]{2,1,0:T(8,128)(2,1)} %get-tuple-element.20.own_ref.refs_0_, bf16[24,32,256]{2,1,0:T(8,128)(2,1)S(1)} %copy-done.3, bf16[24,32,256]{2,1,0:T(8,128)(2,1)S(1)} %copy-done.5, ...), custom_call_target="tpu_custom_call" | custom-call | flops 1 | bytes 1 | tf_op jit(solution)/shard_map/correlate_partial/pallas_call | solution.py:243
  157.4 3.0 %collective-permute-done.9.refs_3_ = bf16[24,32,256]{2,1,0:T(8,128)(2,1)S(1)} collective-permute-done((bf16[24,32,256]{2,1,0:T(8,128)(2,1)S(1)}, bf16[24,32,256]{2,1,0:T(8,128)(2,1)S(1)}, u32[]{:S(2)}, u32[]{:S(2)}) %collective-permute-start.9) | collective-permute-done | bytes 393248 | tf_op jit(solution)/shard_map/ppermute | solution.py:35
  160.6 0.8 collective-permute-start.10
  161.4 3.0 %collective-permute-done.10.refs_5_ = bf16[4,24,32,256]{3,2,1,0:T(8,128)(2,1)S(1)} collective-permute-done((bf16[4,24,32,256]{3,2,1,0:T(8,128)(2,1)S(1)}, bf16[4,24,32,256]{3,2,1,0:T(8,128)(2,1)S(1)}, u32[]{:S(2)}, u32[]{:S(2)}) %collective-permute-start.10) | collective-permute-done | bytes 1572896 | tf_op jit(solution)/shard_map/ppermute | solution.py:39
  164.4 14.1 %correlate_final.1 = f32[1952,128]{1,0:T(8,128)} custom-call(s32[32,128]{1,0:T(8,128)S(1)} %copy-done.8, f32[288,2048]{1,0:T(8,128)S(1)} %get-tuple-element.29.before_ref, bf16[24,304,512]{2,1,0:T(8,128)(2,1)S(1)} %get-tuple-element.30.q_ref, bf16[24,32,256]{2,1,0:T(8,128)(2,1)S(1)} %get-tuple-element.26.own_ref.refs_0_, ...), custom_call_target="tpu_custom_call" | custom-call | flops 1 | bytes 1 | tf_op jit(solution)/shard_map/correlate_final/pallas_call | solution.py:265
  (36 shorter events, 3.2 us)
Async XLA Ops:
  0.7 7.2 %collective-permute-start = (bf16[48,256]{1,0:T(8,128)(2,1)S(1)}, bf16[48,256]{1,0:T(8,128)(2,1)S(1)}, u32[]{:S(2)}, u32[]{:S(2)}) collective-permute-start(bf16[48,256]{1,0:T(8,128)(2,1)S(1)} %slice.3), channel_id=1, source_target_pairs={{1,0},{2,1},{3,2},{4,3},{5,4},{6,5},{7,6},{8,7},{9,8},{10,9},{11,1... | collective-permute-start | bytes 73736 | tf_op jit(solution)/shard_map/ppermute | solution.py:29
  8.0 0.6 copy-start.10
  14.6 11.4 %copy-start.9 = (s32[64,62]{1,0:T(8,128)S(1)}, s32[64,62]{1,0:T(8,128)}, u32[]{:S(2)}) copy-start(s32[64,62]{1,0:T(8,128)} %param.7) | copy-start | bytes 47620
  14.6 11.5 %copy-start.11 = (s32[64]{0:T(128)S(1)}, s32[64]{0:T(128)}, u32[]{:S(2)}) copy-start(s32[64]{0:T(128)} %param.6) | copy-start | bytes 772
  14.7 84.1 %all-to-all-start = ((bf16[64,96,256]{2,1,0:T(8,128)(2,1)}), bf16[64,96,256]{2,1,0:T(8,128)(2,1)S(1)}, u32[]{:S(2)}, u32[]{:S(2)}) async-start(bf16[64,96,256]{2,1,0:T(8,128)(2,1)} %cut_windows.1), calls=%async_computation | async-start | bytes 6291456 | tf_op jit(solution)/shard_map/all_to_all | solution.py:354
  101.8 12.2 %collective-permute-start.1 = (bf16[24,32,256]{2,1,0:T(8,128)(2,1)}, bf16[24,32,256]{2,1,0:T(8,128)(2,1)S(1)}, u32[]{:S(2)}, u32[]{:S(2)}) collective-permute-start(bf16[24,32,256]{2,1,0:T(8,128)(2,1)} %get-tuple-element.20.own_ref.refs_0_), channel_id=1, source_target_pairs={{0,8},{1,9},{2,10},{3,11},{4,12},{5,13},{6,14},{7,15},{8,16},{9,17... | collective-permute-start | bytes 1179656 | tf_op jit(solution)/shard_map/ppermute | solution.py:29
  107.9 3.0 %copy-start = (bf16[24,304,512]{2,1,0:T(8,128)(2,1)}, bf16[24,304,512]{2,1,0:T(8,128)(2,1)S(1)}, u32[]{:S(2)}) copy-start(bf16[24,304,512]{2,1,0:T(8,128)(2,1)S(1)} %get-tuple-element.21.q_ref) | copy-start | bytes 22413316
  110.8 11.9 %collective-permute-start.5 = (bf16[24,32,256]{2,1,0:T(8,128)(2,1)S(1)}, bf16[24,32,256]{2,1,0:T(8,128)(2,1)S(1)}, u32[]{:S(2)}, u32[]{:S(2)}) collective-permute-start(bf16[24,32,256]{2,1,0:T(8,128)(2,1)S(1)} %get-tuple-element.26.own_ref.refs_0_), channel_id=1, source_target_pairs={{0,8},{1,9},{2,10},{3,11},{4,12},{5,13},{6,14},{7,15},{8,16},{9,17... | collective-permute-start | bytes 1179656 | tf_op jit(solution)/shard_map/ppermute | solution.py:29
  115.7 9.2 %collective-permute-start.2 = (bf16[24,32,256]{2,1,0:T(8,128)(2,1)S(1)}, bf16[24,32,256]{2,1,0:T(8,128)(2,1)S(1)}, u32[]{:S(2)}, u32[]{:S(2)}) collective-permute-start(bf16[24,32,256]{2,1,0:T(8,128)(2,1)S(1)} %get-tuple-element.23), channel_id=1, source_target_pairs={{0,2},{1,3},{2,4},{3,5},{4,6},{5,7},{6,0},{7,1},{8,10},{9,11},{10,... | collective-permute-start | bytes 1179656 | tf_op jit(solution)/shard_map/ppermute | solution.py:35
  115.7 10.4 %collective-permute-start.3 = (bf16[24,32,256]{2,1,0:T(8,128)(2,1)S(1)}, bf16[24,32,256]{2,1,0:T(8,128)(2,1)S(1)}, u32[]{:S(2)}, u32[]{:S(2)}) collective-permute-start(bf16[24,32,256]{2,1,0:T(8,128)(2,1)S(1)} %get-tuple-element.24), channel_id=1, source_target_pairs={{0,4},{1,5},{2,6},{3,7},{4,0},{5,1},{6,2},{7,3},{8,12},{9,13},{10,... | collective-permute-start | bytes 1179656 | tf_op jit(solution)/shard_map/ppermute | solution.py:35
  118.0 18.6 %collective-permute-start.4 = (bf16[24,32,256]{2,1,0:T(8,128)(2,1)S(1)}, bf16[24,32,256]{2,1,0:T(8,128)(2,1)S(1)}, u32[]{:S(2)}, u32[]{:S(2)}) collective-permute-start(bf16[24,32,256]{2,1,0:T(8,128)(2,1)S(1)} %get-tuple-element.25), channel_id=1, source_target_pairs={{0,6},{1,7},{2,0},{3,1},{4,2},{5,3},{6,4},{7,5},{8,14},{9,15},{10,... | collective-permute-start | bytes 1179656 | tf_op jit(solution)/shard_map/ppermute | solution.py:35
  124.9 16.6 %copy-start.2 = (bf16[24,32,256]{2,1,0:T(8,128)(2,1)}, bf16[24,32,256]{2,1,0:T(8,128)(2,1)S(1)}, u32[]{:S(2)}) copy-start(bf16[24,32,256]{2,1,0:T(8,128)(2,1)S(1)} %collective-permute-done.2.refs_1_) | copy-start | bytes 1179652
  126.1 15.4 %copy-start.4 = (bf16[24,32,256]{2,1,0:T(8,128)(2,1)}, bf16[24,32,256]{2,1,0:T(8,128)(2,1)S(1)}, u32[]{:S(2)}) copy-start(bf16[24,32,256]{2,1,0:T(8,128)(2,1)S(1)} %collective-permute-done.3.refs_2_) | copy-start | bytes 1179652
  136.6 4.9 %copy-start.6 = (bf16[24,32,256]{2,1,0:T(8,128)(2,1)}, bf16[24,32,256]{2,1,0:T(8,128)(2,1)S(1)}, u32[]{:S(2)}) copy-start(bf16[24,32,256]{2,1,0:T(8,128)(2,1)S(1)} %collective-permute-done.4.refs_3_) | copy-start | bytes 1179652
  137.9 3.6 %collective-permute-start.6 = (bf16[4,24,32,256]{3,2,1,0:T(8,128)(2,1)S(1)}, bf16[4,24,32,256]{3,2,1,0:T(8,128)(2,1)S(1)}, u32[]{:S(2)}, u32[]{:S(2)}) collective-permute-start(bf16[4,24,32,256]{3,2,1,0:T(8,128)(2,1)S(1)} %exchange.2), channel_id=1, source_target_pairs={{0,1},{1,0},{2,3},{3,2},{4,5},{5,4},{6,7},{7,6},{8,9},{9,8},{10,11... | collective-permute-start | bytes 4718600 | tf_op jit(solution)/shard_map/ppermute | solution.py:39
  138.5 18.9 %collective-permute-start.7 = (bf16[24,32,256]{2,1,0:T(8,128)(2,1)S(1)}, bf16[24,32,256]{2,1,0:T(8,128)(2,1)S(1)}, u32[]{:S(2)}, u32[]{:S(2)}) collective-permute-start(bf16[24,32,256]{2,1,0:T(8,128)(2,1)S(1)} %get-tuple-element.31), channel_id=1, source_target_pairs={{0,2},{1,3},{2,4},{3,5},{4,6},{5,7},{6,0},{7,1},{8,10},{9,11},{10,... | collective-permute-start | bytes 1179656 | tf_op jit(solution)/shard_map/ppermute | solution.py:35
  139.5 17.9 %collective-permute-start.8 = (bf16[24,32,256]{2,1,0:T(8,128)(2,1)S(1)}, bf16[24,32,256]{2,1,0:T(8,128)(2,1)S(1)}, u32[]{:S(2)}, u32[]{:S(2)}) collective-permute-start(bf16[24,32,256]{2,1,0:T(8,128)(2,1)S(1)} %get-tuple-element.32), channel_id=1, source_target_pairs={{0,4},{1,5},{2,6},{3,7},{4,0},{5,1},{6,2},{7,3},{8,12},{9,13},{10,... | collective-permute-start | bytes 1179656 | tf_op jit(solution)/shard_map/ppermute | solution.py:35
  141.2 19.3 %collective-permute-start.9 = (bf16[24,32,256]{2,1,0:T(8,128)(2,1)S(1)}, bf16[24,32,256]{2,1,0:T(8,128)(2,1)S(1)}, u32[]{:S(2)}, u32[]{:S(2)}) collective-permute-start(bf16[24,32,256]{2,1,0:T(8,128)(2,1)S(1)} %get-tuple-element.33), channel_id=1, source_target_pairs={{0,6},{1,7},{2,0},{3,1},{4,2},{5,3},{6,4},{7,5},{8,14},{9,15},{10,... | collective-permute-start | bytes 1179656 | tf_op jit(solution)/shard_map/ppermute | solution.py:35
  141.5 3.1 %copy-start.1 = (bf16[24,304,512]{2,1,0:T(8,128)(2,1)S(1)}, bf16[24,304,512]{2,1,0:T(8,128)(2,1)}, u32[]{:S(2)}) copy-start(bf16[24,304,512]{2,1,0:T(8,128)(2,1)} %copy-done) | copy-start | bytes 22413316
  144.6 1.0 copy-start.3
  145.6 1.0 copy-start.5
  146.6 1.0 copy-start.7
  157.4 7.0 %copy-start.8 = (s32[32,128]{1,0:T(8,128)S(1)}, s32[32,128]{1,0:T(8,128)}, u32[]{:S(2)}) copy-start(s32[32,128]{1,0:T(8,128)} %neighbours_ref.1) | copy-start | bytes 49156
  160.6 3.8 %collective-permute-start.10 = (bf16[4,24,32,256]{3,2,1,0:T(8,128)(2,1)S(1)}, bf16[4,24,32,256]{3,2,1,0:T(8,128)(2,1)S(1)}, u32[]{:S(2)}, u32[]{:S(2)}) collective-permute-start(bf16[4,24,32,256]{3,2,1,0:T(8,128)(2,1)S(1)} %exchange.3), channel_id=1, source_target_pairs={{0,1},{1,0},{2,3},{3,2},{4,5},{5,4},{6,7},{7,6},{8,9},{9,8},{10,11... | collective-permute-start | bytes 4718600 | tf_op jit(solution)/shard_map/ppermute | solution.py:39

commit v3 on v2

--- a/solution.py
+++ b/solution.py
@@ -250,7 +250,9 @@
         + [pl.BlockSpec(memory_space=pl.ANY)] * len(after),
         out_specs=[sums, pl.BlockSpec(TOKEN.shape, lambda c: (0, 0))],
         scratch_shapes=[pltpu.VMEM((rows, WIN), jnp.bfloat16)],
-        cost_estimate=LITTLE,
+        cost_estimate=pl.CostEstimate(
+            flops=2 * components * rows * WIN * STEPS * width, bytes_accessed=12 * 2**20, transcendentals=0
+        ),
         compiler_params=pltpu.CompilerParams(vmem_limit_bytes=VMEM_LIMIT),
         name="correlate_partial",
     )(q, *before, *pieces, *after)
@@ -279,7 +281,9 @@
             pltpu.VMEM((tiles, STEPS * width, LANE), jnp.float32),
             pltpu.VMEM((STEPS * width, k), jnp.float32),
         ],
-        cost_estimate=LITTLE,
+        cost_estimate=pl.CostEstimate(
+            flops=2 * components * rows * WIN * STEPS * width, bytes_accessed=12 * 2**20, transcendentals=0
+        ),
         compiler_params=pltpu.CompilerParams(vmem_limit_bytes=VMEM_LIMIT),
         name="correlate_final",
     )(neighbours, before, q, *pieces)

time: 181 us -> 177 us (0.978)
  Pallas kernels: 42.8 us -> 38.1 us
  waiting for transfers between devices: 97.9 us -> 102 us
    ppermute x6, waiting for transfers between devices: 16.8 us -> 20 us  [along_row(): lax.ppermute(array, 'ev', [(i, i // row * row + (i % row + 2 * by) % row)...]
    unnamed x25 -> x17, local copies, waits for them, and re-layouts: 9.76 us -> 8.52 us
  transfers between devices with their start and end apart: 12 -> 12, of which waited for: 10 -> 10; matrix products, arithmetic and copies ran while one was open for 2% -> 2% of each run, Pallas kernels for 10% -> 8%
where the time goes in v3:
time: 177 us; the launch traced here: 176 us
  waiting for transfers between devices  102 us (58%)
  Pallas kernels  38.1 us (22%)
  starting transfers between devices  23 us (13%)
  local copies, waits for them, and re-layouts  10.5 us (6%)
    all_to_all x1, waiting for transfers between devices, body(): lax.all_to_all(bucket, 'ev', split_axis=0, concat_axis=0, tiled=True)  72 us
    ppermute x6, waiting for transfers between devices, along_row(): lax.ppermute(array, 'ev', [(i, i // row * row + (i % row + 2 * by) % row)...  20 us
    pallas_call x1, Pallas kernels, correlate_final(): pl.pallas_call(final_kernel, out_shape=jax.ShapeDtypeStruct((LAGS * event...  14.1 us
    all_to_all x1, starting transfers between devices, body(): lax.all_to_all(bucket, 'ev', split_axis=0, concat_axis=0, tiled=True)  10.3 us
    pallas_call x1, Pallas kernels, correlate_partial(): pl.pallas_call(functools.partial(partial_kernel, len(before), len(pieces)...  8.94 us
    unnamed x17, local copies, waits for them, and re-layouts  8.52 us
    ppermute x3, waiting for transfers between devices, from_behind(): return lax.ppermute(array, axis, pairs)  7 us
    pallas_call x1, Pallas kernels, cut_windows(): pl.pallas_call(cut_kernel, out_shape=jax.ShapeDtypeStruct((devices, 2 * c...  6.66 us
  transfers between devices with their start and end apart: 12, of which 10 were waited for; matrix products, arithmetic and copies ran while one was open for 2% of the time, Pallas kernels for 8%

profile of v3, /device:TPU:57, one launch (start us, length us, event | category | flops | bytes accessed | tf_op | source)
XLA Modules:
  0.0 176.0 jit_solution(7164044753251092511)
XLA Ops:
  0.0 0.7 slice.3
  0.7 2.6 %collective-permute-start = (bf16[48,256]{1,0:T(8,128)(2,1)S(1)}, bf16[48,256]{1,0:T(8,128)(2,1)S(1)}, u32[]{:S(2)}, u32[]{:S(2)}) collective-permute-start(bf16[48,256]{1,0:T(8,128)(2,1)S(1)} %slice.3), channel_id=1, source_target_pairs={{1,0},{2,1},{3,2},{4,3},{5,4},{6,5},{7,6},{8,7},{9,8},{10,9},{11,1... | collective-permute-start | bytes 73736 | tf_op jit(solution)/shard_map/ppermute | solution.py:29
  3.3 1.2 and_select_fusion.owner_ref
  4.5 1.2 dynamic_slice.9.count_ref
  5.7 2.3 %collective-permute-done.rim_ref = bf16[48,256]{1,0:T(8,128)(2,1)S(1)} collective-permute-done((bf16[48,256]{1,0:T(8,128)(2,1)S(1)}, bf16[48,256]{1,0:T(8,128)(2,1)S(1)}, u32[]{:S(2)}, u32[]{:S(2)}) %collective-permute-start) | collective-permute-done | bytes 24608 | tf_op jit(solution)/shard_map/ppermute | solution.py:29
  8.0 0.6 copy-done.6
  8.6 6.7 %cut_windows.1 = bf16[64,96,256]{2,1,0:T(8,128)(2,1)} custom-call(s32[62]{0:T(128)} %bitcast.14, s32[62]{0:T(128)} %and_select_fusion.owner_ref, s32[1]{0:T(128)} %dynamic_slice.9.count_ref, bf16[48,8192]{1,0:T(8,128)(2,1)} %traces_ref.1, bf16[48,256]{1,0:T(8,128)(2,1)} %copy-done.6), custom_call_target="tpu_custom_call" | custom-call | flops 1 | bytes 1 | tf_op jit(solution)/shard_map/cut_windows/pallas_call | solution.py:65
  15.3 10.3 %all-to-all-start = ((bf16[64,96,256]{2,1,0:T(8,128)(2,1)}), bf16[64,96,256]{2,1,0:T(8,128)(2,1)S(1)}, u32[]{:S(2)}, u32[]{:S(2)}) async-start(bf16[64,96,256]{2,1,0:T(8,128)(2,1)} %cut_windows.1), calls=%async_computation | async-start | bytes 6291456 | tf_op jit(solution)/shard_map/all_to_all | solution.py:358
  26.2 72.0 %all-to-all-done.arrived_ref = bf16[64,96,256]{2,1,0:T(8,128)(2,1)S(1)} async-done(((bf16[64,96,256]{2,1,0:T(8,128)(2,1)}), bf16[64,96,256]{2,1,0:T(8,128)(2,1)S(1)}, u32[]{:S(2)}, u32[]{:S(2)}) %all-to-all-start) | async-done | bytes 3145760 | tf_op jit(solution)/shard_map/all_to_all | solution.py:358
  98.3 2.3 %pick_own.1 = (bf16[24,32,256]{2,1,0:T(8,128)(2,1)S(1)}, bf16[24,32,256]{2,1,0:T(8,128)(2,1)S(1)}) custom-call(s32[32]{0:T(128)S(1)} %select_reduce_fusion.source_ref, bf16[64,96,256]{2,1,0:T(8,128)(2,1)S(1)} %all-to-all-done.arrived_ref), custom_call_target="tpu_custom_call" | custom-call | flops 1 | bytes 1 | tf_op jit(solution)/shard_map/pick_own/pallas_call | solution.py:99
  100.6 0.7 copy-done
  101.3 1.9 %collective-permute-start.1 = (bf16[24,32,256]{2,1,0:T(8,128)(2,1)S(1)}, bf16[24,32,256]{2,1,0:T(8,128)(2,1)S(1)}, u32[]{:S(2)}, u32[]{:S(2)}) collective-permute-start(bf16[24,32,256]{2,1,0:T(8,128)(2,1)S(1)} %get-tuple-element.20.own_ref.refs_0_), channel_id=1, source_target_pairs={{0,8},{1,9},{2,10},{3,11},{4,12},{5,13},{6,14},{7,15},{8,16},{9,17... | collective-permute-start | bytes 1179656 | tf_op jit(solution)/shard_map/ppermute | solution.py:29
  103.3 2.4 %shifted.2 = (bf16[24,304,512]{2,1,0:T(8,128)(2,1)S(1)}, f32[8,128]{1,0:T(8,128)S(1)}) custom-call(bf16[24,32,256]{2,1,0:T(8,128)(2,1)S(1)} %get-tuple-element.20.own_ref.refs_0_), custom_call_target="tpu_custom_call" | custom-call | flops 1 | bytes 1 | tf_op jit(solution)/shard_map/shifted/pallas_call | solution.py:142
  105.7 2.9 %copy-done.2 = bf16[24,304,512]{2,1,0:T(8,128)(2,1)} copy-done((bf16[24,304,512]{2,1,0:T(8,128)(2,1)}, bf16[24,304,512]{2,1,0:T(8,128)(2,1)S(1)}, u32[]{:S(2)}) %copy-start.2) | copy-done | bytes 7471128
  108.7 1.9 %collective-permute-start.5 = (bf16[24,32,256]{2,1,0:T(8,128)(2,1)}, bf16[24,32,256]{2,1,0:T(8,128)(2,1)S(1)}, u32[]{:S(2)}, u32[]{:S(2)}) collective-permute-start(bf16[24,32,256]{2,1,0:T(8,128)(2,1)} %copy-done), channel_id=1, source_target_pairs={{0,8},{1,9},{2,10},{3,11},{4,12},{5,13},{6,14},{7,15},{8,16},{9,17... | collective-permute-start | bytes 1179656 | tf_op jit(solution)/shard_map/ppermute | solution.py:29
  110.6 2.7 %collective-permute-done.1.above_ref.refs_4_ = bf16[24,32,256]{2,1,0:T(8,128)(2,1)S(1)} collective-permute-done((bf16[24,32,256]{2,1,0:T(8,128)(2,1)S(1)}, bf16[24,32,256]{2,1,0:T(8,128)(2,1)S(1)}, u32[]{:S(2)}, u32[]{:S(2)}) %collective-permute-start.1) | collective-permute-done | bytes 393248 | tf_op jit(solution)/shard_map/ppermute | solution.py:29
  113.3 0.9 along_rows.2
  114.2 2.3 %collective-permute-start.3 = (bf16[24,32,256]{2,1,0:T(8,128)(2,1)S(1)}, bf16[24,32,256]{2,1,0:T(8,128)(2,1)S(1)}, u32[]{:S(2)}, u32[]{:S(2)}) collective-permute-start(bf16[24,32,256]{2,1,0:T(8,128)(2,1)S(1)} %get-tuple-element.24), channel_id=1, source_target_pairs={{0,4},{1,5},{2,6},{3,7},{4,0},{5,1},{6,2},{7,3},{8,12},{9,13},{10,... | collective-permute-start | bytes 1179656 | tf_op jit(solution)/shard_map/ppermute | solution.py:35
  116.5 1.0 copy-done.1
  117.5 2.4 %shifted.3 = (bf16[24,304,512]{2,1,0:T(8,128)(2,1)S(1)}, f32[8,128]{1,0:T(8,128)S(1)}) custom-call(bf16[24,32,256]{2,1,0:T(8,128)(2,1)S(1)} %copy-done.1), custom_call_target="tpu_custom_call" | custom-call | flops 1 | bytes 1 | tf_op jit(solution)/shard_map/shifted/pallas_call | solution.py:142
  120.0 2.0 %collective-permute-done.5.above_ref.refs_4_ = bf16[24,32,256]{2,1,0:T(8,128)(2,1)S(1)} collective-permute-done((bf16[24,32,256]{2,1,0:T(8,128)(2,1)}, bf16[24,32,256]{2,1,0:T(8,128)(2,1)S(1)}, u32[]{:S(2)}, u32[]{:S(2)}) %collective-permute-start.5) | collective-permute-done | bytes 393248 | tf_op jit(solution)/shard_map/ppermute | solution.py:29
  122.1 0.7 collective-permute-done.2.refs_1_
  122.8 1.0 collective-permute-done.3.refs_2_
  123.8 11.4 %collective-permute-done.4.refs_3_ = bf16[24,32,256]{2,1,0:T(8,128)(2,1)S(1)} collective-permute-done((bf16[24,32,256]{2,1,0:T(8,128)(2,1)S(1)}, bf16[24,32,256]{2,1,0:T(8,128)(2,1)S(1)}, u32[]{:S(2)}, u32[]{:S(2)}) %collective-permute-start.4) | collective-permute-done | bytes 393248 | tf_op jit(solution)/shard_map/ppermute | solution.py:35
  135.9 1.1 collective-permute-start.7
  137.0 1.6 collective-permute-start.8
  138.9 3.1 %copy-done.3 = bf16[24,304,512]{2,1,0:T(8,128)(2,1)S(1)} copy-done((bf16[24,304,512]{2,1,0:T(8,128)(2,1)S(1)}, bf16[24,304,512]{2,1,0:T(8,128)(2,1)}, u32[]{:S(2)}) %copy-start.3) | copy-done | bytes 7471128
  142.0 8.9 %correlate_partial.1 = (f32[288,2048]{1,0:T(8,128)S(1)}, f32[8,128]{1,0:T(8,128)S(1)}) custom-call(bf16[24,304,512]{2,1,0:T(8,128)(2,1)S(1)} %copy-done.3, bf16[24,32,256]{2,1,0:T(8,128)(2,1)S(1)} %get-tuple-element.20.own_ref.refs_0_, bf16[24,32,256]{2,1,0:T(8,128)(2,1)S(1)} %collective-permute-done.2.refs_1_, ...), custom_call_target="tpu_custom_call" | custom-call | flops 7247757312 | bytes 12582912 | tf_op jit(solution)/shard_map/correlate_partial/pallas_call | solution.py:243
  151.0 6.9 %collective-permute-done.9.refs_3_ = bf16[24,32,256]{2,1,0:T(8,128)(2,1)S(1)} collective-permute-done((bf16[24,32,256]{2,1,0:T(8,128)(2,1)S(1)}, bf16[24,32,256]{2,1,0:T(8,128)(2,1)S(1)}, u32[]{:S(2)}, u32[]{:S(2)}) %collective-permute-start.9) | collective-permute-done | bytes 393248 | tf_op jit(solution)/shard_map/ppermute | solution.py:35
  158.0 0.8 collective-permute-start.10
  158.8 3.0 %collective-permute-done.10.refs_5_ = bf16[4,24,32,256]{3,2,1,0:T(8,128)(2,1)S(1)} collective-permute-done((bf16[4,24,32,256]{3,2,1,0:T(8,128)(2,1)S(1)}, bf16[4,24,32,256]{3,2,1,0:T(8,128)(2,1)S(1)}, u32[]{:S(2)}, u32[]{:S(2)}) %collective-permute-start.10) | collective-permute-done | bytes 1572896 | tf_op jit(solution)/shard_map/ppermute | solution.py:39
  161.8 14.1 %correlate_final.1 = f32[1952,128]{1,0:T(8,128)} custom-call(s32[32,128]{1,0:T(8,128)S(1)} %copy-done.4, f32[288,2048]{1,0:T(8,128)S(1)} %get-tuple-element.29.before_ref, bf16[24,304,512]{2,1,0:T(8,128)(2,1)S(1)} %get-tuple-element.30.q_ref, bf16[24,32,256]{2,1,0:T(8,128)(2,1)S(1)} %copy-done.1, bf16[24,32,256]{2,1,0:T(8,128)(2,1)S(1)} %collective-permute-done.7.refs_1_, ...), custom_call_target="tpu_custom_call" | custom-call | flops 7247757312 | bytes 12582912 | tf_op jit(solution)/shard_map/correlate_final/pallas_call | solution.py:267
  (28 shorter events, 1.9 us)
Async XLA Ops:
  0.7 7.2 %collective-permute-start = (bf16[48,256]{1,0:T(8,128)(2,1)S(1)}, bf16[48,256]{1,0:T(8,128)(2,1)S(1)}, u32[]{:S(2)}, u32[]{:S(2)}) collective-permute-start(bf16[48,256]{1,0:T(8,128)(2,1)S(1)} %slice.3), channel_id=1, source_target_pairs={{1,0},{2,1},{3,2},{4,3},{5,4},{6,5},{7,6},{8,7},{9,8},{10,9},{11,1... | collective-permute-start | bytes 73736 | tf_op jit(solution)/shard_map/ppermute | solution.py:29
  8.0 0.6 copy-start.6
  15.3 10.3 %copy-start.5 = (s32[64,62]{1,0:T(8,128)S(1)}, s32[64,62]{1,0:T(8,128)}, u32[]{:S(2)}) copy-start(s32[64,62]{1,0:T(8,128)} %param.7) | copy-start | bytes 47620
  15.3 10.4 %copy-start.7 = (s32[64]{0:T(128)S(1)}, s32[64]{0:T(128)}, u32[]{:S(2)}) copy-start(s32[64]{0:T(128)} %param.6) | copy-start | bytes 772
  15.3 83.0 %all-to-all-start = ((bf16[64,96,256]{2,1,0:T(8,128)(2,1)}), bf16[64,96,256]{2,1,0:T(8,128)(2,1)S(1)}, u32[]{:S(2)}, u32[]{:S(2)}) async-start(bf16[64,96,256]{2,1,0:T(8,128)(2,1)} %cut_windows.1), calls=%async_computation | async-start | bytes 6291456 | tf_op jit(solution)/shard_map/all_to_all | solution.py:358
  100.6 0.8 copy-start
  101.3 12.0 %collective-permute-start.1 = (bf16[24,32,256]{2,1,0:T(8,128)(2,1)S(1)}, bf16[24,32,256]{2,1,0:T(8,128)(2,1)S(1)}, u32[]{:S(2)}, u32[]{:S(2)}) collective-permute-start(bf16[24,32,256]{2,1,0:T(8,128)(2,1)S(1)} %get-tuple-element.20.own_ref.refs_0_), channel_id=1, source_target_pairs={{0,8},{1,9},{2,10},{3,11},{4,12},{5,13},{6,14},{7,15},{8,16},{9,17... | collective-permute-start | bytes 1179656 | tf_op jit(solution)/shard_map/ppermute | solution.py:29
  105.7 3.0 %copy-start.2 = (bf16[24,304,512]{2,1,0:T(8,128)(2,1)}, bf16[24,304,512]{2,1,0:T(8,128)(2,1)S(1)}, u32[]{:S(2)}) copy-start(bf16[24,304,512]{2,1,0:T(8,128)(2,1)S(1)} %get-tuple-element.21.q_ref) | copy-start | bytes 22413316
  108.7 13.3 %collective-permute-start.5 = (bf16[24,32,256]{2,1,0:T(8,128)(2,1)}, bf16[24,32,256]{2,1,0:T(8,128)(2,1)S(1)}, u32[]{:S(2)}, u32[]{:S(2)}) collective-permute-start(bf16[24,32,256]{2,1,0:T(8,128)(2,1)} %copy-done), channel_id=1, source_target_pairs={{0,8},{1,9},{2,10},{3,11},{4,12},{5,13},{6,14},{7,15},{8,16},{9,17... | collective-permute-start | bytes 1179656 | tf_op jit(solution)/shard_map/ppermute | solution.py:29
  114.2 8.6 %collective-permute-start.2 = (bf16[24,32,256]{2,1,0:T(8,128)(2,1)}, bf16[24,32,256]{2,1,0:T(8,128)(2,1)S(1)}, u32[]{:S(2)}, u32[]{:S(2)}) collective-permute-start(bf16[24,32,256]{2,1,0:T(8,128)(2,1)} %get-tuple-element.23), channel_id=1, source_target_pairs={{0,2},{1,3},{2,4},{3,5},{4,6},{5,7},{6,0},{7,1},{8,10},{9,11},{10,... | collective-permute-start | bytes 1179656 | tf_op jit(solution)/shard_map/ppermute | solution.py:35
  114.2 9.6 %collective-permute-start.3 = (bf16[24,32,256]{2,1,0:T(8,128)(2,1)S(1)}, bf16[24,32,256]{2,1,0:T(8,128)(2,1)S(1)}, u32[]{:S(2)}, u32[]{:S(2)}) collective-permute-start(bf16[24,32,256]{2,1,0:T(8,128)(2,1)S(1)} %get-tuple-element.24), channel_id=1, source_target_pairs={{0,4},{1,5},{2,6},{3,7},{4,0},{5,1},{6,2},{7,3},{8,12},{9,13},{10,... | collective-permute-start | bytes 1179656 | tf_op jit(solution)/shard_map/ppermute | solution.py:35
  116.5 18.6 %collective-permute-start.4 = (bf16[24,32,256]{2,1,0:T(8,128)(2,1)S(1)}, bf16[24,32,256]{2,1,0:T(8,128)(2,1)S(1)}, u32[]{:S(2)}, u32[]{:S(2)}) collective-permute-start(bf16[24,32,256]{2,1,0:T(8,128)(2,1)S(1)} %get-tuple-element.25), channel_id=1, source_target_pairs={{0,6},{1,7},{2,0},{3,1},{4,2},{5,3},{6,4},{7,5},{8,14},{9,15},{10,... | collective-permute-start | bytes 1179656 | tf_op jit(solution)/shard_map/ppermute | solution.py:35
  116.5 1.0 copy-start.1
  135.3 3.6 %collective-permute-start.6 = (bf16[4,24,32,256]{3,2,1,0:T(8,128)(2,1)S(1)}, bf16[4,24,32,256]{3,2,1,0:T(8,128)(2,1)S(1)}, u32[]{:S(2)}, u32[]{:S(2)}) collective-permute-start(bf16[4,24,32,256]{3,2,1,0:T(8,128)(2,1)S(1)} %exchange.2), channel_id=1, source_target_pairs={{0,1},{1,0},{2,3},{3,2},{4,5},{5,4},{6,7},{7,6},{8,9},{9,8},{10,11... | collective-permute-start | bytes 4718600 | tf_op jit(solution)/shard_map/ppermute | solution.py:39
  135.9 15.1 %collective-permute-start.7 = (bf16[24,32,256]{2,1,0:T(8,128)(2,1)S(1)}, bf16[24,32,256]{2,1,0:T(8,128)(2,1)S(1)}, u32[]{:S(2)}, u32[]{:S(2)}) collective-permute-start(bf16[24,32,256]{2,1,0:T(8,128)(2,1)S(1)} %get-tuple-element.31), channel_id=1, source_target_pairs={{0,2},{1,3},{2,4},{3,5},{4,6},{5,7},{6,0},{7,1},{8,10},{9,11},{10,... | collective-permute-start | bytes 1179656 | tf_op jit(solution)/shard_map/ppermute | solution.py:35
  137.0 14.0 %collective-permute-start.8 = (bf16[24,32,256]{2,1,0:T(8,128)(2,1)S(1)}, bf16[24,32,256]{2,1,0:T(8,128)(2,1)S(1)}, u32[]{:S(2)}, u32[]{:S(2)}) collective-permute-start(bf16[24,32,256]{2,1,0:T(8,128)(2,1)S(1)} %get-tuple-element.32), channel_id=1, source_target_pairs={{0,4},{1,5},{2,6},{3,7},{4,0},{5,1},{6,2},{7,3},{8,12},{9,13},{10,... | collective-permute-start | bytes 1179656 | tf_op jit(solution)/shard_map/ppermute | solution.py:35
  138.5 19.4 %collective-permute-start.9 = (bf16[24,32,256]{2,1,0:T(8,128)(2,1)S(1)}, bf16[24,32,256]{2,1,0:T(8,128)(2,1)S(1)}, u32[]{:S(2)}, u32[]{:S(2)}) collective-permute-start(bf16[24,32,256]{2,1,0:T(8,128)(2,1)S(1)} %get-tuple-element.33), channel_id=1, source_target_pairs={{0,6},{1,7},{2,0},{3,1},{4,2},{5,3},{6,4},{7,5},{8,14},{9,15},{10,... | collective-permute-start | bytes 1179656 | tf_op jit(solution)/shard_map/ppermute | solution.py:35
  138.9 3.1 %copy-start.3 = (bf16[24,304,512]{2,1,0:T(8,128)(2,1)S(1)}, bf16[24,304,512]{2,1,0:T(8,128)(2,1)}, u32[]{:S(2)}) copy-start(bf16[24,304,512]{2,1,0:T(8,128)(2,1)} %copy-done.2) | copy-start | bytes 22413316
  151.0 10.9 %copy-start.4 = (s32[32,128]{1,0:T(8,128)S(1)}, s32[32,128]{1,0:T(8,128)}, u32[]{:S(2)}) copy-start(s32[32,128]{1,0:T(8,128)} %neighbours_ref.1) | copy-start | bytes 49156
  158.0 3.8 %collective-permute-start.10 = (bf16[4,24,32,256]{3,2,1,0:T(8,128)(2,1)S(1)}, bf16[4,24,32,256]{3,2,1,0:T(8,128)(2,1)S(1)}, u32[]{:S(2)}, u32[]{:S(2)}) collective-permute-start(bf16[4,24,32,256]{3,2,1,0:T(8,128)(2,1)S(1)} %exchange.3), channel_id=1, source_target_pairs={{0,1},{1,0},{2,3},{3,2},{4,5},{5,4},{6,7},{7,6},{8,9},{9,8},{10,11... | collective-permute-start | bytes 4718600 | tf_op jit(solution)/shard_map/ppermute | solution.py:39
